TPU v7x, 32 devices: a whole 2x2x4 slice. The times are simulated.
32 devices in a mesh: dp: 4 (over z), node: 8 (over y, x, core).
Axes of the slice: x: 2, y: 2, z: 4, core: 2. Of those that a mesh axis runs over, the one named last changes fastest.
Arguments:
- node_state: bfloat16 [4, 4, 1024, 512], P('dp', None, 'node'), may hold values from -6 to 6
- edge_state: bfloat16 [4, 4, 6144, 512], P('dp', None, 'node'), may hold values from -6 to 6
- node_cotangent: bfloat16 [4, 4, 1024, 512], P('dp', None, 'node'), may hold values from -6 to 6
- edge_cotangent: bfloat16 [4, 4, 6144, 512], P('dp', None, 'node'), may hold values from -6 to 6
- send_rows: int32 [8, 64], P('node'), may hold values from 0 to 127
- edge_sender: int32 [6144], P('node'), may hold values from 0 to 191
- edge_receiver: int32 [6144], P('node'), may hold values from 0 to 127
- rollout_length: int32 [4], P('dp'), may hold values from 1 to 4, as said below
- slot_block: int32 [8], replicated, may hold values from 0 to 7, each once
- step_count: int32 [9], replicated, may hold values from 2 to 6
- weight_slots: float32 [8, 512, 512], P('dp', 'node'), may hold values from -0.1875 to 0.1875
- moment_first: float32 [8, 512, 512], P('dp', 'node'), may hold values from -6 to 6
- moment_second: float32 [8, 512, 512], P('dp', 'node'), may hold values from 0.5 to 3
- basis_left: float32 [8, 512, 512], P('dp', None, 'node'), may hold values from -1 to 1, as said below
- basis_right: float32 [8, 512, 512], P('dp'), may hold values from -1 to 1, as said below
- vector_params: float32 [8, 512], replicated
- vector_first: float32 [8, 512], replicated, may hold values from -6 to 6
- vector_second: float32 [8, 512], replicated, may hold values from 0.5 to 3
Outputs:
- node_output: bfloat16 [4, 4, 1024, 512], P('dp', None, 'node')
- edge_output: bfloat16 [4, 4, 6144, 512], P('dp', None, 'node')
- node_gradient: bfloat16 [4, 4, 1024, 512], P('dp', None, 'node')
- edge_gradient: bfloat16 [4, 4, 6144, 512], P('dp', None, 'node')
- new_first: float32 [8, 512, 512], P('dp', 'node')
- new_second: float32 [8, 512, 512], P('dp', 'node')
- new_weights: float32 [8, 512, 512], P('dp', 'node')
- weights_copy: bfloat16 [8, 512, 512], P('dp', 'node')
- vector_state: float32 [3, 8, 512], replicated
- global_norm: float32 [1], replicated
Inputs may be any that keep to these rules, and one draw needn't show every extreme that they name: Slot s holds weight block slot_block[s] where that is below 7, and no block otherwise. `rollout_length`: some sample has all 4 steps. `basis_left`: each slot's matrix is orthogonal. `basis_right`: each slot's matrix is orthogonal.
All inputs are finite; a program needn't handle non-finite values.
Results may differ from a plain program's by a relative error of at most 0.0095.
Values may be sent and summed in bfloat16 or wider, within the bound.
A program may use at most 192 MiB of HBM per device.

v0:
```python
import functools
import math

import jax
import jax.numpy as jnp
from jax import lax
from jax.experimental import pallas as pl
from jax.experimental.pallas import tpu as pltpu
from jax.sharding import PartitionSpec as P

NBLOCK = 7
f32 = jnp.float32
bf16 = jnp.bfloat16
highest = lax.Precision.HIGHEST
norm_epsilon = 1e-05
adam_epsilon = 1e-08
beta_first = 0.5
beta_second = 0.5
rate_matrix = 0.03
rate_vector = 0.4
weight_decay = 0.01


def dot(a, b):
    return jnp.dot(a, b, preferred_element_type=f32)


def dot_tb(a, b):
    return lax.dot_general(a, b, (((1,), (1,)), ((), ())), preferred_element_type=f32)


def dot_ta(a, b):
    return lax.dot_general(a, b, (((0,), (0,)), ((), ())), preferred_element_type=f32)


def eights(x):
    return jnp.sum(x.reshape(x.shape[0] // 8, 8, x.shape[1]), axis=0)


def sigmoid(z):
    return 0.5 * jnp.tanh(0.5 * z) + 0.5


def branch_forward(z, w_out, bias_out):
    s = sigmoid(z)
    h = z * s
    slope = s + h * (1.0 - s)
    hidden = h.astype(bf16)
    after = dot(hidden, w_out) + bias_out
    center = after - jnp.mean(after, axis=1, keepdims=True)
    spread = jnp.mean(center * center, axis=1, keepdims=True)
    inverse = lax.rsqrt(spread + norm_epsilon)
    return hidden, slope, center * inverse, inverse


def norm_backward(upstream, normed, inverse, gain):
    u = upstream * gain
    first = jnp.mean(u, axis=1, keepdims=True)
    second = jnp.mean(u * normed, axis=1, keepdims=True)
    return (inverse * (u - first - normed * second)).astype(bf16)


def layer_kernel(
    rollout_ref,
    slot_block_ref,
    node_hbm,
    edge_hbm,
    ncot_hbm,
    ecot_hbm,
    sender_ref,
    receiver_ref,
    halo_ref,
    w_ref,
    vec_ref,
    nout_ref,
    eout_hbm,
    nbase_ref,
    egrad_hbm,
    grad_ref,
    gvec_ref,
    hback_ref,
    node_v,
    edge_v,
    ncot_v,
    ecot_v,
    eout_v,
    egrad_v,
    gather_t,
    gather,
    table,
    hidden_v,
    slope_v,
    normed_v,
    inv_v,
    dz_v,
    da_v,
    summed_v,
    dsum_v,
    sc_own,
    sc_recv,
    sc_halo,
    acc,
    sem_in,
    sem_out,
):
    roll, nodes, width = node_v.shape
    edges = edge_v.shape[1]
    peers, per_peer = sc_halo.shape[0], sc_halo.shape[2]
    halo = peers * per_peer
    known = nodes + halo
    padded = table.shape[1]
    chunk = 256
    pieces = edges // chunk

    copies = []
    for i, (src, dst) in enumerate(
        ((node_hbm, node_v), (edge_hbm, edge_v), (ncot_hbm, ncot_v), (ecot_hbm, ecot_v))
    ):
        copies.append(pltpu.make_async_copy(src.at[0], dst, sem_in.at[i]))
        copies[-1].start()

    slot_of = []
    for b in range(NBLOCK):
        found = jnp.int32(0)
        for s in range(slot_block_ref.shape[0]):
            found = jnp.where(slot_block_ref[s] == b, jnp.int32(s), found)
        slot_of.append(found)

    def weight(b):
        return w_ref[slot_of[b]]

    def live(t):
        return jnp.where(t < rollout_ref[0], 1.0, 0.0).astype(f32)

    ids = lax.broadcasted_iota(jnp.int32, (padded, edges), 0)
    onehot = (ids == sender_ref[...]) | (ids == receiver_ref[...] + known)
    onehot = jnp.where(onehot, 1.0, 0.0).astype(f32)
    gather_t[...] = onehot.astype(bf16)
    gather[...] = onehot.T.astype(bf16)
    table[...] = jnp.zeros_like(table)
    acc[...] = jnp.zeros_like(acc)

    copies[0].wait()
    flat_nodes = node_v[...].reshape(roll * nodes, width)
    own_sent = dot(flat_nodes, weight(1))
    own_recv = dot(flat_nodes, weight(2))
    halo_sent = dot(halo_ref[...], weight(1)).reshape(peers, roll, per_peer, width)
    for t in range(roll):
        table[t, :nodes] = own_sent[t * nodes : (t + 1) * nodes].astype(bf16)
        table[t, nodes:known] = halo_sent[:, t].reshape(halo, width).astype(bf16)
        table[t, known : known + nodes] = own_recv[t * nodes : (t + 1) * nodes].astype(bf16)
    copies[1].wait()

    def forward(t, carry):
        lv = live(t)
        total = jnp.zeros((nodes, width), f32)
        for c in range(pieces):
            rows = pl.ds(c * chunk, chunk)
            edge = edge_v[t, rows]
            z = dot(edge, weight(0)) + dot(gather[rows], table[t]) + vec_ref[0:1]
            hidden, slope, normed, inverse = branch_forward(z, weight(3), vec_ref[1:2])
            hidden_v[t, rows] = hidden
            slope_v[t, rows] = slope.astype(bf16)
            normed_v[t, rows] = normed.astype(bf16)
            inv_v[t, rows] = inverse
            new = edge.astype(f32) + (normed * vec_ref[2:3] + vec_ref[3:4])
            eout_v[t, rows] = (new * lv).astype(bf16)
            total += dot(gather_t[known : known + nodes, rows], new.astype(bf16))
        summed_v[pl.ds(t * nodes, nodes)] = total.astype(bf16)
        pltpu.make_async_copy(eout_v.at[t], eout_hbm.at[0, t], sem_out.at[t]).start()
        return carry

    lax.fori_loop(0, roll, forward, 0)

    flat_nodes = node_v[...].reshape(roll * nodes, width)
    summed = summed_v[...]
    z = dot(flat_nodes, weight(4)) + dot(summed, weight(5)) + vec_ref[4:5]
    hidden, slope, normed, inverse = branch_forward(z, weight(6), vec_ref[5:6])
    row_t = lax.broadcasted_iota(jnp.int32, (roll * nodes, 1), 0) // nodes
    row_live = jnp.where(row_t < rollout_ref[0], 1.0, 0.0).astype(f32)
    new = flat_nodes.astype(f32) + (normed * vec_ref[6:7] + vec_ref[7:8])
    nout_ref[0] = (new * row_live).astype(bf16).reshape(roll, nodes, width)
    copies[2].wait()
    d_new = ncot_v[...].reshape(roll * nodes, width).astype(f32) * row_live
    acc[6] += eights(d_new * normed)
    acc[7] += eights(d_new)
    d_after = norm_backward(d_new, normed, inverse, vec_ref[6:7])
    acc[5] += eights(d_after.astype(f32))
    grad_ref[6] = dot_ta(hidden, d_after)
    d_before = (dot_tb(d_after, weight(6)) * slope).astype(bf16)
    acc[4] += eights(d_before.astype(f32))
    grad_ref[4] = dot_ta(flat_nodes, d_before)
    grad_ref[5] = dot_ta(summed, d_before)
    dsum_v[...] = dot_tb(d_before, weight(5)).astype(bf16)
    nbase_ref[...] = d_new + dot_tb(d_before, weight(4))
    grad_ref[0] = jnp.zeros((width, width), f32)
    grad_ref[3] = jnp.zeros((width, width), f32)
    copies[3].wait()

    def backward(t, carry):
        lv = live(t)
        for c in range(pieces):
            rows = pl.ds(c * chunk, chunk)
            d_new = ecot_v[t, rows].astype(f32) * lv + dot(
                gather[rows, known : known + nodes], dsum_v[pl.ds(t * nodes, nodes)]
            )
            normed = normed_v[t, rows].astype(f32)
            acc[2] += eights(d_new * normed)
            acc[3] += eights(d_new)
            d_after = norm_backward(d_new, normed, inv_v[t, rows], vec_ref[2:3])
            acc[1] += eights(d_after.astype(f32))
            da_v[rows] = d_after
            d_before = (dot_tb(d_after, weight(3)) * slope_v[t, rows].astype(f32)).astype(bf16)
            acc[0] += eights(d_before.astype(f32))
            dz_v[rows] = d_before
            egrad_v[t, rows] = (d_new + dot_tb(d_before, weight(0))).astype(bf16)
        pltpu.make_async_copy(egrad_v.at[t], egrad_hbm.at[0, t], sem_out.at[roll + t]).start()
        grad_ref[3] += dot_ta(hidden_v[t], da_v[...])
        grad_ref[0] += dot_ta(edge_v[t], dz_v[...])
        scattered = dot(gather_t[...], dz_v[...])
        sc_own[pl.ds(t * nodes, nodes)] = scattered[:nodes].astype(bf16)
        sc_recv[pl.ds(t * nodes, nodes)] = scattered[known : known + nodes].astype(bf16)
        sc_halo[:, t] = scattered[nodes:known].reshape(peers, per_peer, width)
        return carry

    lax.fori_loop(0, roll, backward, 0)

    halo_sum = sc_halo[...].reshape(roll * halo, width).astype(bf16)
    grad_ref[1] = dot_ta(flat_nodes, sc_own[...]) + dot_ta(halo_ref[...], halo_sum)
    grad_ref[2] = dot_ta(flat_nodes, sc_recv[...])
    hback_ref[...] = dot_tb(halo_sum, weight(1)).astype(bf16)
    nbase_ref[...] += dot_tb(sc_own[...], weight(1)) + dot_tb(sc_recv[...], weight(2))
    gvec_ref[...] = jnp.sum(acc[...], axis=1)

    for t in range(roll):
        pltpu.make_async_copy(eout_v.at[t], eout_hbm.at[0, t], sem_out.at[t]).wait()
        pltpu.make_async_copy(egrad_v.at[t], egrad_hbm.at[0, t], sem_out.at[roll + t]).wait()


def layer(
    rollout_length,
    slot_block,
    node_state,
    edge_state,
    node_cotangent,
    edge_cotangent,
    edge_sender,
    edge_receiver,
    halo,
    slots,
    vector_params,
    per_peer,
):
    _, roll, nodes, width = node_state.shape
    edges = edge_state.shape[2]
    peers = halo.shape[0] // (roll * per_peer)
    known = nodes + peers * per_peer
    padded = -(-(known + nodes) // 128) * 128
    vmem = pl.BlockSpec(memory_space=pltpu.VMEM)
    smem = pl.BlockSpec(memory_space=pltpu.SMEM)
    hbm = pl.BlockSpec(memory_space=pl.ANY)
    shape = jax.ShapeDtypeStruct
    return pl.pallas_call(
        layer_kernel,
        out_shape=(
            shape(node_state.shape, bf16),
            shape(edge_state.shape, bf16),
            shape((roll * nodes, width), f32),
            shape(edge_state.shape, bf16),
            shape((NBLOCK, width, width), f32),
            shape((8, width), f32),
            shape(halo.shape, bf16),
        ),
        in_specs=[smem, smem, hbm, hbm, hbm, hbm, vmem, vmem, vmem, vmem, vmem],
        out_specs=(vmem, hbm, vmem, hbm, vmem, vmem, vmem),
        scratch_shapes=[
            pltpu.VMEM((roll, nodes, width), bf16),
            pltpu.VMEM((roll, edges, width), bf16),
            pltpu.VMEM((roll, nodes, width), bf16),
            pltpu.VMEM((roll, edges, width), bf16),
            pltpu.VMEM((roll, edges, width), bf16),
            pltpu.VMEM((roll, edges, width), bf16),
            pltpu.VMEM((padded, edges), bf16),
            pltpu.VMEM((edges, padded), bf16),
            pltpu.VMEM((roll, padded, width), bf16),
            pltpu.VMEM((roll, edges, width), bf16),
            pltpu.VMEM((roll, edges, width), bf16),
            pltpu.VMEM((roll, edges, width), bf16),
            pltpu.VMEM((roll, edges, 1), f32),
            pltpu.VMEM((edges, width), bf16),
            pltpu.VMEM((edges, width), bf16),
            pltpu.VMEM((roll * nodes, width), bf16),
            pltpu.VMEM((roll * nodes, width), bf16),
            pltpu.VMEM((roll * nodes, width), bf16),
            pltpu.VMEM((roll * nodes, width), bf16),
            pltpu.VMEM((peers, roll, per_peer, width), f32),
            pltpu.VMEM((8, 8, width), f32),
            pltpu.SemaphoreType.DMA((4,)),
            pltpu.SemaphoreType.DMA((2 * roll,)),
        ],
        compiler_params=pltpu.CompilerParams(vmem_limit_bytes=60 << 20),
        name="layer",
    )(
        rollout_length,
        slot_block,
        node_state,
        edge_state,
        node_cotangent,
        edge_cotangent,
        edge_sender.reshape(1, edges),
        edge_receiver.reshape(1, edges),
        halo,
        slots,
        vector_params,
    )


def adam_direction(moment_one, moment_two, fix_one, fix_two):
    return moment_one / fix_one / (jnp.sqrt(moment_two / fix_two) + adam_epsilon)


def local(
    node_state,
    edge_state,
    node_cotangent,
    edge_cotangent,
    send_rows,
    edge_sender,
    edge_receiver,
    rollout_length,
    slot_block,
    step_count,
    weight_slots,
    moment_first,
    moment_second,
    basis_left,
    basis_right,
    vector_params,
    vector_first,
    vector_second,
):
    width = node_state.shape[-1]
    roll, nodes = node_state.shape[1:3]
    clip_limit = math.sqrt(NBLOCK * width * width + 8 * width)
    slot_dev = weight_slots.shape[0]
    slot_total = slot_block.shape[0]
    halo_rows = send_rows.shape[1]
    peers = lax.axis_size("node")
    per_peer = halo_rows // peers
    copies = lax.all_gather(weight_slots.astype(bf16), "node", axis=1, tiled=True)
    slots = lax.all_gather(copies, "dp", axis=0, tiled=True)
    back_onehot = (send_rows[0][:, None] == jnp.arange(nodes, dtype=jnp.int32)[None, :]).astype(bf16)
    outgoing = jnp.einsum("hk,tkd->htd", back_onehot, node_state[0], preferred_element_type=f32)
    outgoing = outgoing.astype(bf16).reshape(peers, per_peer, roll, width).transpose(0, 2, 1, 3)
    outgoing = outgoing.reshape(peers * roll * per_peer, width)
    halo = lax.all_to_all(outgoing, "node", split_axis=0, concat_axis=0, tiled=True)

    node_output, edge_output, node_base, edge_gradient, grads, grad_vectors, halo_back = layer(
        rollout_length,
        slot_block,
        node_state,
        edge_state,
        node_cotangent,
        edge_cotangent,
        edge_sender,
        edge_receiver,
        halo,
        slots,
        vector_params,
        per_peer,
    )
    returned = lax.all_to_all(halo_back, "node", split_axis=0, concat_axis=0, tiled=True)
    returned = returned.reshape(peers, roll, per_peer, width).transpose(0, 2, 1, 3)
    d_back = jnp.einsum(
        "hk,htd->tkd",
        back_onehot,
        returned.reshape(halo_rows, roll, width),
        preferred_element_type=f32,
    )
    node_gradient = node_base.reshape(roll, nodes, width) + d_back
    node_gradient = node_gradient.astype(bf16).reshape(node_state.shape)

    block_of_slot = slot_block[None, :] == jnp.arange(NBLOCK, dtype=jnp.int32)[:, None]
    first = lax.axis_index("dp") * slot_dev
    summed, grad_vectors = lax.psum((grads, grad_vectors), ("dp", "node"))
    own_square = jnp.sum(summed * summed)
    mine = lax.dynamic_slice_in_dim(block_of_slot.astype(f32), first, slot_dev, 1)
    owned_grads = jnp.einsum("bs,bij->sij", mine, summed, precision=highest)
    square_sum = own_square + jnp.sum(grad_vectors * grad_vectors)
    grad_norm = jnp.sqrt(square_sum)
    clip_scale = jnp.minimum(1.0, clip_limit / grad_norm)
    owned_grads = owned_grads * clip_scale
    grad_vectors = grad_vectors * clip_scale
    own_steps = lax.dynamic_slice_in_dim(step_count, first, slot_dev, 0)
    slot_steps = own_steps.astype(f32)[:, None, None]
    fix_one = 1.0 - jnp.power(f32(beta_first), slot_steps)
    fix_two = 1.0 - jnp.power(f32(beta_second), slot_steps)
    rotated = jnp.einsum("sij,sik->sjk", basis_left, owned_grads, precision=highest, preferred_element_type=f32)
    rotated = jnp.einsum("sjk,skl->sjl", rotated, basis_right, precision=highest, preferred_element_type=f32)
    moment_one = beta_first * moment_first + (1.0 - beta_first) * rotated
    moment_two = beta_second * moment_second + (1.0 - beta_second) * rotated * rotated
    direction = adam_direction(moment_one, moment_two, fix_one, fix_two)
    turned = jnp.einsum("sjl,sml->sjm", direction, basis_right, precision=highest, preferred_element_type=f32)
    reverted = jnp.einsum("sij,sjm->ism", basis_left, turned, precision=highest, preferred_element_type=f32)
    reverted = lax.psum_scatter(reverted.astype(bf16), "node", scatter_dimension=0, tiled=True).astype(f32)
    reverted = jnp.transpose(reverted, (1, 0, 2))
    new_weights = weight_slots - rate_matrix * (reverted + weight_decay * weight_slots)
    vec_step = step_count[slot_total].astype(f32)
    vfix_one = 1.0 - jnp.power(f32(beta_first), vec_step)
    vfix_two = 1.0 - jnp.power(f32(beta_second), vec_step)
    vec_one = beta_first * vector_first + (1.0 - beta_first) * grad_vectors
    vec_two = beta_second * vector_second + (1.0 - beta_second) * grad_vectors * grad_vectors
    vec_new = vector_params - rate_vector * adam_direction(vec_one, vec_two, vfix_one, vfix_two)
    vector_state = jnp.stack([vec_new, vec_one, vec_two])
    return (
        node_output,
        edge_output,
        node_gradient,
        edge_gradient,
        moment_one,
        moment_two,
        new_weights,
        new_weights.astype(bf16),
        vector_state,
        grad_norm.reshape(1),
    )


def solution(mesh):
    in_specs = (
        P("dp", None, "node", None),
        P("dp", None, "node", None),
        P("dp", None, "node", None),
        P("dp", None, "node", None),
        P("node", None),
        P("node"),
        P("node"),
        P("dp"),
        P(),
        P(),
        P("dp", "node", None),
        P("dp", "node", None),
        P("dp", "node", None),
        P("dp", None, "node"),
        P("dp", None, None),
        P(),
        P(),
        P(),
    )
    out_specs = (
        P("dp", None, "node", None),
        P("dp", None, "node", None),
        P("dp", None, "node", None),
        P("dp", None, "node", None),
        P("dp", "node", None),
        P("dp", "node", None),
        P("dp", "node", None),
        P("dp", "node", None),
        P(),
        P(),
    )
    return jax.shard_map(local, mesh=mesh, in_specs=in_specs, out_specs=out_specs, check_vma=False)
```

profile of v0, /device:TPU:1, one launch (start us, length us, event | category | flops | bytes accessed | tf_op | source)
XLA Modules:
  0.0 422.7 jit_solution(13058300773063686204)
XLA Ops:
  7.2 0.0 copy-start
  7.2 0.0 copy-start.12
  7.2 0.0 copy-start.13
  7.2 0.0 all-gather.3.cloned.1.call-start
  7.3 1.8 convert_element_type.29
  9.0 0.0 all-gather.3.cloned.1.call-update
  9.0 0.0 all-gather.5.cloned.1.call-start
  9.1 27.5 %all-gather.3.cloned.1.call-done = bf16[2,512,512]{2,1,0:T(8,128)(2,1)} async-done(((bf16[2,64,512]{2,1,0:T(8,128)(2,1)}), bf16[2,512,512]{2,1,0:T(8,128)(2,1)}) %all-gather.3.cloned.1.call-update) | async-done | bytes 1048592 | tf_op jit(solution)/shard_map/all_gather | solution.py:350
  36.6 0.0 all-gather.5.cloned.1.call-update
  36.6 1.3 fusion.7
  37.9 0.7 copy.58
  38.7 3.6 all-to-all-start
  42.2 0.0 all-reduce.4.cloned.1.call-start
  42.9 0.0 copy-done.12
  42.9 0.6 reshape.61.sender_ref
  43.5 0.0 copy-done.13
  43.5 0.6 reshape.62.receiver_ref
  44.0 3.8 all-to-all-done
  47.9 70.6 %all-gather.5.cloned.1.call-done.w_ref = bf16[8,512,512]{2,1,0:T(8,128)(2,1)} async-done(((bf16[2,512,512]{2,1,0:T(8,128)(2,1)}), bf16[8,512,512]{2,1,0:T(8,128)(2,1)}) %all-gather.5.cloned.1.call-update) | async-done | bytes 4194320 | tf_op jit(solution)/shard_map/all_gather | solution.py:351
  118.5 39.9 %layer.1 = (bf16[1,4,128,512]{3,2,1,0:T(8,128)(2,1)}, bf16[1,4,768,512]{3,2,1,0:T(8,128)(2,1)}, f32[512,512]{1,0:T(8,128)}, bf16[1,4,768,512]{3,2,1,0:T(8,128)(2...) custom-call(s32[1]{0:T(128)S(6)} %copy.61.rollout_ref, s32[8]{0:T(128)} %slot_block_ref.1, ...), custom_call_target="tpu_custom_call" | custom-call | tf_op jit(solution)/shard_map/layer/pallas_call | solution.py:263
  158.4 0.0 copy-start.16
  158.4 0.0 copy-start.15
  158.5 0.0 copy-start.11
  158.5 0.0 all-reduce.4.cloned.1.call-update
  158.5 0.6 copy-done.16
  159.1 0.1 power_subtract_fusion
  159.2 0.0 copy-done.15
  159.2 4.6 %all-to-all-start.1 = ((bf16[8,32,512]{2,1,0:T(8,128)(2,1)}), bf16[8,32,512]{2,1,0:T(8,128)(2,1)}, u32[]{:S(2)}, u32[]{:S(2)}) async-start(bf16[8,32,512]{2,1,0:T(8,128)(2,1)} %bitcast.8), calls=%async_computation.1 | async-start | bytes 524288 | tf_op jit(solution)/shard_map/all_to_all | solution.py:372
  163.8 42.0 %psum.15 = f32[8,512]{1,0:T(8,128)S(1)} all-reduce(f32[8,512]{1,0:T(8,128)S(1)} %copy-done.11), channel_id=1, replica_groups=mesh['dp'=4,'node'=8] {'dp','node'}, use_global_device_ids=true, to_apply=%region_2.0 | all-reduce | flops 4096 | bytes 32768 | tf_op jit(solution)/shard_map/psum | solution.py:385
  205.8 0.6 multiply_reduce_fusion.1
  206.4 120.5 %all-reduce.4.cloned.1.call-done = f32[7,512,512]{2,1,0:T(8,128)} async-done(((f32[7,512,512]{2,1,0:T(8,128)}), f32[7,512,512]{2,1,0:T(8,128)}) %all-reduce.4.cloned.1.call-update) | async-done | bytes 7340048 | tf_op jit(solution)/shard_map/psum | solution.py:385
  326.9 5.6 %multiply_reduce_fusion = f32[]{:T(128)} fusion(f32[7,512,512]{2,1,0:T(8,128)} %all-reduce.4.cloned.1.call-done), kind=kLoop, calls=%fused_computation.2 | loop fusion | flops 3670015 | bytes 7340036 | tf_op jit(solution)/shard_map/reduce_sum | solution.py:386
  333.9 0.0 copy-start.5
  333.9 12.7 %fusion = f32[2,512,512]{2,0,1:T(2,128)S(1)} fusion(f32[7,512,512]{2,1,0:T(8,128)} %all-reduce.4.cloned.1.call-done, pred[7,8]{1,0:T(8,128)(4,1)S(1)} %iota_compare_fusion.1, s32[]{:T(128)S(6)} %select_n.6), kind=kOutput, calls=%fused_computation | convolution fusion | flops 44040192 | bytes 9437244 | tf_op jit(solution)/shard_map/bs,bij->sij/dot_general | solution.py:388
  346.6 0.0 copy-done.5
  346.6 0.0 copy-start.6
  346.6 0.0 copy-start.7
  346.6 1.6 fusion.2
  348.3 1.4 fusion.10
  349.7 0.0 copy-start.3
  349.7 0.0 copy-start.4
  349.7 0.7 copy-done.3
  350.4 2.1 fusion.15
  352.5 0.0 copy-start.17
  352.5 1.8 fusion.3
  354.3 2.1 copy.39
  356.4 0.0 all-reduce.6.cloned.1.call-update
  356.5 0.6 slice.3
  357.7 0.6 dynamic-slice
  359.0 0.0 copy-start.8
  359.0 0.0 copy-start.9
  359.0 0.0 copy-start.10
  359.0 0.0 copy-start.2
  359.0 1.6 copy.38
  360.6 0.0 all-to-all-done.1
  360.7 2.1 fusion.6
  362.7 2.0 copy.42
  364.8 0.0 copy-done.9
  364.8 0.6 pad_maximum_fusion
  365.5 46.8 %all-reduce.6.cloned.1.call-done = bf16[512,2,512]{2,1,0:T(2,128)(2,1)} async-done(((bf16[512,2,512]{2,1,0:T(2,128)(2,1)}), bf16[512,2,512]{2,1,0:T(2,128)(2,1)}) %all-reduce.6.cloned.1.call-update) | async-done | bytes 1048592
  412.3 0.0 copy-done.2
  412.3 1.3 fusion.35
  413.6 0.8 copy.43
  414.4 0.7 copy.44
  (15 shorter events, 0.1 us)
Async XLA Ops:
  7.2 341.1 %copy-start = (f32[2,512,512]{2,1,0:T(8,128)S(1)}, f32[2,512,512]{2,1,0:T(8,128)}, u32[]{:S(2)}) copy-start(f32[2,512,512]{2,1,0:T(8,128)} %param.32) | copy-start | bytes 6291460
  7.2 35.7 %copy-start.12 = (s32[768]{0:T(1024)S(1)}, s32[768]{0:T(1024)}, u32[]{:S(2)}) copy-start(s32[768]{0:T(1024)} %param.23) | copy-start | bytes 9220
  7.2 36.3 %copy-start.13 = (s32[768]{0:T(1024)S(1)}, s32[768]{0:T(1024)}, u32[]{:S(2)}) copy-start(s32[768]{0:T(1024)} %param.24) | copy-start | bytes 9220
  7.2 29.4 %all-gather.3.cloned.1.call-start = ((), (), s32[]{:S(2)}) async-start(), calls=%async_computation.2 | async-start | bytes 1179648 | tf_op jit(solution)/shard_map/all_gather | solution.py:350
  9.0 109.5 %all-gather.5.cloned.1.call-start = ((), (), s32[]{:S(2)}) async-start(), calls=%async_computation.3 | async-start | bytes 5242880 | tf_op jit(solution)/shard_map/all_gather | solution.py:351
  38.7 9.2 %all-to-all-start = ((bf16[8,32,512]{2,1,0:T(8,128)(2,1)}), bf16[8,32,512]{2,1,0:T(8,128)(2,1)S(1)}, u32[]{:S(2)}, u32[]{:S(2)}) async-start(bf16[8,32,512]{2,1,0:T(8,128)(2,1)} %bitcast.63), calls=%async_computation | async-start | bytes 524288 | tf_op jit(solution)/shard_map/all_to_all | solution.py:356
  42.2 284.7 %all-reduce.4.cloned.1.call-start = ((), (), s32[]{:S(2)}) async-start(), calls=%async_computation.4 | async-start | bytes 14680064 | tf_op jit(solution)/shard_map/psum | solution.py:385
  47.9 70.6 %copy-start.1 = (bf16[8,32,512]{2,1,0:T(8,128)(2,1)}, bf16[8,32,512]{2,1,0:T(8,128)(2,1)S(1)}, u32[]{:S(2)}) copy-start(bf16[8,32,512]{2,1,0:T(8,128)(2,1)S(1)} %all-to-all-done) | copy-start | bytes 786436
  158.4 0.7 copy-start.16
  158.4 0.7 copy-start.15
  158.5 5.3 %copy-start.11 = (f32[8,512]{1,0:T(8,128)S(1)}, f32[8,512]{1,0:T(8,128)}, u32[]{:S(2)}) copy-start(f32[8,512]{1,0:T(8,128)} %get-tuple-element.23) | copy-start | bytes 49156
  159.2 201.5 %all-to-all-start.1 = ((bf16[8,32,512]{2,1,0:T(8,128)(2,1)}), bf16[8,32,512]{2,1,0:T(8,128)(2,1)}, u32[]{:S(2)}, u32[]{:S(2)}) async-start(bf16[8,32,512]{2,1,0:T(8,128)(2,1)} %bitcast.8), calls=%async_computation.1 | async-start | bytes 524288 | tf_op jit(solution)/shard_map/all_to_all | solution.py:372
  163.8 248.5 %all-reduce.6.cloned.1.call-start = ((), (), s32[]{:S(2)}) async-start(), calls=%async_computation.5 | async-start | bytes 2097152
  333.9 12.7 %copy-start.5 = (f32[2,512,64]{1,2,0:T(8,128)S(1)}, f32[2,512,64]{1,2,0:T(8,128)}, u32[]{:S(2)}) copy-start(f32[2,512,64]{1,2,0:T(8,128)} %param.31) | copy-start | bytes 786436
  346.6 1.7 copy-start.6
  346.6 1.7 copy-start.7
  349.7 0.7 copy-start.3
  349.7 2.8 copy-start.4
  352.5 5.2 %copy-start.17 = (u32[32]{0:T(128)S(1)}, u32[32]{0:T(128)}, u32[]{:S(2)}) copy-start(u32[32]{0:T(128)} %constant.51) | copy-start | bytes 388
  356.4 4.2 %copy-start.14 = (s32[1,64]{1,0:T(1,128)S(1)}, s32[1,64]{1,0:T(1,128)}, u32[]{:S(2)}) copy-start(s32[1,64]{1,0:T(1,128)} %param.22) | copy-start | bytes 772
  359.0 5.8 %copy-start.8 = (f32[8,512]{1,0:T(8,128)S(1)}, f32[8,512]{1,0:T(8,128)}, u32[]{:S(2)}) copy-start(f32[8,512]{1,0:T(8,128)} %vec_ref.1) | copy-start | bytes 49156
  359.0 5.8 %copy-start.9 = (f32[8,512]{1,0:T(8,128)S(1)}, f32[8,512]{1,0:T(8,128)}, u32[]{:S(2)}) copy-start(f32[8,512]{1,0:T(8,128)} %param.34) | copy-start | bytes 49156
  359.0 5.8 %copy-start.10 = (f32[8,512]{1,0:T(8,128)S(1)}, f32[8,512]{1,0:T(8,128)}, u32[]{:S(2)}) copy-start(f32[8,512]{1,0:T(8,128)} %param.35) | copy-start | bytes 49156
  359.0 53.3 %copy-start.2 = (f32[2,64,512]{2,1,0:T(8,128)S(1)}, f32[2,64,512]{2,1,0:T(8,128)}, u32[]{:S(2)}) copy-start(f32[2,64,512]{2,1,0:T(8,128)} %param.28) | copy-start | bytes 786436
Sparse Core Ops, SparseCore 0:
  10.5 25.9 all-gather.2
  38.1 80.3 all-gather.4
  158.6 168.2 all-reduce.3
  356.6 55.6 all-reduce.5
where the time goes:
time: 425 us; the launch traced here: 423 us
  waiting for transfers between devices  269 us (63%)
  blocking collectives  42 us (10%)
  Pallas kernels  39.9 us (9%)
  matrix products  23.1 us (5%)
  between operations  18.6 us (4%)
  local copies, waits for them, and re-layouts  11.6 us (3%)
  other arithmetic  9.97 us (2%)
  starting transfers between devices  8.24 us (2%)
    psum x1, waiting for transfers between devices, local(): summed, grad_vectors = lax.psum((grads, grad_vectors), ('dp', 'node'))  121 us
    all_gather x1, waiting for transfers between devices, local(): slots = lax.all_gather(copies, 'dp', axis=0, tiled=True)  70.6 us
    unnamed x5, waiting for transfers between devices  46.9 us
    psum x1, blocking collectives, local(): summed, grad_vectors = lax.psum((grads, grad_vectors), ('dp', 'node'))  42 us
    pallas_call x1, Pallas kernels, layer(): pl.pallas_call(layer_kernel, out_shape=(shape(node_state.shape, bf16), sh...  39.9 us
    all_gather x1, waiting for transfers between devices, local(): lax.all_gather(weight_slots.astype(bf16), 'node', axis=1, tiled=True)  27.5 us
    dot_general x1, matrix products, local(): owned_grads = jnp.einsum('bs,bij->sij', mine, summed, precision=highest)  12.7 us
  transfers between devices with their start and end apart: 6, of which 5 were waited for; matrix products, arithmetic and copies ran while one was open for 9% of the time, Pallas kernels for 0%

commit v1 on v0

--- a/solution.py
+++ b/solution.py
@@ -319,6 +319,645 @@
     return moment_one / fix_one / (jnp.sqrt(moment_two / fix_two) + adam_epsilon)
 
 
+MESH = pl.DeviceIdType.MESH
+
+
+class Place:
+    def __init__(self):
+        self.z = lax.axis_index("dp")
+        self.n = lax.axis_index("node")
+        self.c = lax.rem(self.n, 2)
+        self.x = lax.rem(self.n // 2, 2)
+        self.y = self.n // 4
+        self.xn = self.n + 2 - 4 * self.x
+        self.yn = self.n + 4 - 8 * self.y
+        self.sib = self.n + 1 - 2 * self.c
+        self.diag = self.xn + 4 - 8 * self.y
+
+
+def remote(src, dst, send, recv, z, n):
+    return pltpu.make_async_remote_copy(
+        src_ref=src, dst_ref=dst, send_sem=send, recv_sem=recv, device_id=(z, n), device_id_type=MESH
+    )
+
+
+def greet(p, depth, peers):
+    barrier = pltpu.get_barrier_semaphore()
+    for k in range(1, peers):
+        to = lax.rem(p.n + k, peers)
+        pl.semaphore_signal(barrier, inc=1, device_id=(p.z, to), device_id_type=MESH)
+    for k in range(1, depth):
+        to = lax.rem(p.z + k, depth)
+        pl.semaphore_signal(barrier, inc=1, device_id=(to, p.n), device_id_type=MESH)
+    pl.semaphore_wait(barrier, peers + depth - 2)
+
+
+ORDER = ((0, 1, 2, 3), (1, 0, 2, 3), (2, 3, 1, 0), (3, 2, 1, 0))
+
+
+def gather_start(p, buf, k, sems):
+    send, recv = sems
+    own = buf(k, p.n)
+    copies = []
+    for i, to in ((0, p.xn), (1, p.yn), (3, p.sib)):
+        copies.append(remote(own, own, send.at[i, k], recv.at[i, k], p.z, to))
+        copies[-1].start()
+    return copies
+
+
+def gather_side(p, buf, k, sems):
+    send, recv = sems
+    copies = []
+    for i, owner in ((0, p.xn), (1, p.yn)):
+        got = buf(k, owner)
+        remote(got, got, send.at[i, k], recv.at[i, k], p.z, owner).wait_recv()
+        on = remote(got, got, send.at[4 + i, k], recv.at[4 + i, k], p.z, p.sib)
+        on.start()
+        copies.append(on)
+        over = remote(got, got, send.at[2, k], recv.at[2, k], p.z, p.yn if i == 0 else p.xn)
+        pl.when(p.c == i)(over.start)
+    copies.append(over)
+    return copies
+
+
+def gather_far(p, buf, k, sems):
+    send, recv = sems
+    got = buf(k, p.diag)
+    remote(got, got, send.at[2, k], recv.at[2, k], p.z, p.xn).wait_recv()
+    on = remote(got, got, send.at[6, k], recv.at[6, k], p.z, p.sib)
+    on.start()
+    return [on]
+
+
+def gather_end(p, buf, k, sems):
+    send, recv = sems
+    for i in (3, 4, 5, 6):
+        got = buf(k, p.sib)
+        remote(got, got, send.at[i, k], recv.at[i, k], p.z, p.sib).wait_recv()
+
+
+def prepare_kernel(
+    weight_ref,
+    node_ref,
+    send_rows_ref,
+    left_ref,
+    slots,
+    halo,
+    left_t,
+    hout32,
+    hout,
+    left_b,
+    ssem,
+    rsem,
+    zssem,
+    zrsem,
+    hssem,
+    hrsem,
+    lssem,
+    lrsem,
+):
+    p = Place()
+    depth, peers = 4, 8
+    roll, nodes, width = node_ref.shape[1:]
+    slot_dev, rows = weight_ref.shape[:2]
+    per_peer = send_rows_ref.shape[1] // peers
+
+    def buf(k, n):
+        return slots.at[pl.ds(slot_dev * k, slot_dev), n]
+
+    slots[pl.ds(slot_dev * p.z, slot_dev), p.n] = weight_ref[...].astype(bf16)
+    greet(p, depth, peers)
+    going = []
+    order = []
+
+    def arrive(j):
+        k = jnp.int32(0)
+        for z in range(depth):
+            k = k + jnp.where(p.z == z, ORDER[z][j], 0)
+        order.append(k)
+        piece = buf(k, p.n)
+        if j:
+            remote(piece, piece, zssem.at[0, k], zrsem.at[k], p.z, p.n).wait_recv()
+        for i, test, to in (
+            (0, (k <= p.z) & (p.z < depth - 1), p.z + 1),
+            (1, (k >= p.z) & (p.z > 0), p.z - 1),
+        ):
+            copy = remote(piece, piece, zssem.at[i, k], zrsem.at[k], to, p.n)
+            pl.when(test)(copy.start)
+            going.append((copy, test))
+        going.extend((copy, None) for copy in gather_start(p, buf, k, (ssem, rsem)))
+
+    def side(j):
+        going.extend((copy, None) for copy in gather_side(p, buf, order[j], (ssem, rsem)))
+
+    def far(j):
+        going.extend((copy, None) for copy in gather_far(p, buf, order[j], (ssem, rsem)))
+
+    arrive(0)
+    ids = lax.broadcasted_iota(jnp.int32, (nodes, per_peer * peers), 0)
+    pick_t = jnp.where(ids == send_rows_ref[...], 1.0, 0.0).astype(bf16)
+    for t in range(roll):
+        hout32[:, t] = dot_ta(pick_t, node_ref[0, t]).reshape(peers, per_peer, width)
+    hout[...] = hout32[...].reshape(peers, roll * per_peer, width).astype(bf16)
+    halo[p.n] = hout[p.n]
+    for s in range(slot_dev):
+        for m in range(peers):
+            left_b[s, m] = left_ref[s, m * rows : (m + 1) * rows].T.astype(bf16)
+    left_t[:, p.n] = left_b[:, p.n]
+    for k in range(1, peers):
+        to = lax.rem(p.n + k, peers)
+        for copy in (
+            remote(hout.at[to], halo.at[p.n], hssem.at[k], hrsem.at[k], p.z, to),
+            remote(left_b.at[:, to], left_t.at[:, p.n], lssem.at[k], lrsem.at[k], p.z, to),
+        ):
+            copy.start()
+            going.append((copy, None))
+
+    arrive(1)
+    side(0)
+    arrive(2)
+    side(1)
+    far(0)
+    arrive(3)
+    side(2)
+    far(1)
+    side(3)
+    far(2)
+    far(3)
+    for j in range(depth):
+        gather_end(p, buf, order[j], (ssem, rsem))
+    for k in range(1, peers):
+        remote(hout.at[0], halo.at[0], hssem.at[k], hrsem.at[k], p.z, p.sib).wait_recv()
+        remote(left_b.at[:, 0], left_t.at[:, 0], lssem.at[k], lrsem.at[k], p.z, p.sib).wait_recv()
+    for copy, test in going:
+        if test is None:
+            copy.wait_send()
+        else:
+            pl.when(test)(copy.wait_send)
+
+
+def prepare(weight_slots, node_state, send_rows, basis_left):
+    depth, peers = 4, 8
+    _, roll, nodes, width = node_state.shape
+    slot_dev, rows = weight_slots.shape[:2]
+    per_peer = send_rows.shape[1] // peers
+    vmem = pl.BlockSpec(memory_space=pltpu.VMEM)
+    shape = jax.ShapeDtypeStruct
+    dma = pltpu.SemaphoreType.DMA
+    slots, halo, left_t = pl.pallas_call(
+        prepare_kernel,
+        out_shape=(
+            shape((slot_dev * depth, peers, rows, width), bf16),
+            shape((peers, roll * per_peer, width), bf16),
+            shape((slot_dev, peers, rows, rows), bf16),
+        ),
+        in_specs=[vmem] * 4,
+        out_specs=(vmem, vmem, vmem),
+        scratch_shapes=[
+            pltpu.VMEM((peers, roll, per_peer, width), f32),
+            pltpu.VMEM((peers, roll * per_peer, width), bf16),
+            pltpu.VMEM((slot_dev, peers, rows, rows), bf16),
+            dma((7, depth)),
+            dma((7, depth)),
+            dma((2, depth)),
+            dma((depth,)),
+            dma((peers,)),
+            dma((peers,)),
+            dma((peers,)),
+            dma((peers,)),
+        ],
+        compiler_params=pltpu.CompilerParams(
+            vmem_limit_bytes=40 << 20, collective_id=0, has_side_effects=True
+        ),
+        name="prepare",
+    )(weight_slots, node_state, send_rows, basis_left)
+    return (
+        slots.reshape(slot_dev * depth, width, width),
+        halo.reshape(peers * roll * per_peer, width),
+        left_t.reshape(slot_dev, width, rows),
+    )
+
+
+def update_kernel(
+    slot_block_ref,
+    step_ref,
+    grad_ref,
+    gvec_ref,
+    hback_ref,
+    nbase_ref,
+    send_rows_ref,
+    weight_ref,
+    first_ref,
+    second_ref,
+    left_ref,
+    right_ref,
+    left_t_ref,
+    vec_ref,
+    vfirst_ref,
+    vsecond_ref,
+    ngrad_ref,
+    mone_ref,
+    mtwo_ref,
+    wnew_ref,
+    wcopy_ref,
+    vstate_ref,
+    norm_ref,
+    cast,
+    got_core,
+    put_one,
+    keep_one,
+    got_one,
+    put_two,
+    keep_two,
+    got_two,
+    plane,
+    put_up,
+    put_down,
+    got_up,
+    got_down,
+    full,
+    turned,
+    hret,
+    vput,
+    vgot,
+    vz,
+    sput,
+    sgot,
+    szput,
+    sz,
+    ssem,
+    rsem,
+    gssem,
+    grsem,
+    tssem,
+    trsem,
+    zssem,
+    zrsem,
+    hssem,
+    hrsem,
+    vssem,
+    vrsem,
+    nssem,
+    nrsem,
+):
+    p = Place()
+    depth, peers = 4, 8
+    slot_dev, rows, width = weight_ref.shape
+    roll = ngrad_ref.shape[1]
+    nodes = ngrad_ref.shape[2]
+    per_peer = hback_ref.shape[1] // roll
+    on_f = jnp.where(p.c == 0, p.x, p.y)
+    on_g = jnp.where(p.c == 0, p.y, p.x)
+    to_f = jnp.where(p.c == 0, p.xn, p.yn)
+    to_g = jnp.where(p.c == 0, p.yn, p.xn)
+    going = []
+
+    def launch(src, dst, send, recv, z, n):
+        copy = remote(src, dst, send, recv, z, n)
+        copy.start()
+        going.append((copy, None))
+
+    def landed(dst, recv):
+        remote(dst, dst, recv, recv, p.z, p.sib).wait_recv()
+
+    greet(p, depth, peers)
+
+    def to_core(b):
+        cast[b] = grad_ref[b].reshape(peers // 2, 2, rows, width).astype(bf16)
+        launch(cast.at[b, :, 1 - p.c], got_core.at[b], ssem.at[0, b], rsem.at[0, b], p.z, p.sib)
+
+    def to_first(b):
+        landed(got_core.at[b], rsem.at[0, b])
+        for f in range(2):
+            for g in range(2):
+                at = jnp.where(p.c == 0, g * 2 + f, f * 2 + g)
+                own = grad_ref[b, at * 2 + p.c]
+                total = own + got_core[b, at].astype(f32)
+                put_one[b, f, g] = total.astype(bf16)
+
+                @pl.when(on_f == f)
+                def _():
+                    keep_one[b, g] = total
+
+        launch(put_one.at[b, 1 - on_f], got_one.at[b], ssem.at[1, b], rsem.at[1, b], p.z, to_f)
+
+    def to_second(b):
+        landed(got_one.at[b], rsem.at[1, b])
+        put_two[b] = (keep_one[b, 1 - on_g] + got_one[b, 1 - on_g].astype(f32)).astype(bf16)
+        launch(put_two.at[b], got_two.at[b], ssem.at[2, b], rsem.at[2, b], p.z, to_g)
+        keep_two[b] = keep_one[b, on_g] + got_one[b, on_g].astype(f32)
+
+    def settle(b):
+        landed(got_two.at[b], rsem.at[2, b])
+        plane[b] = keep_two[b] + got_two[b].astype(f32)
+
+    for k in range(1, peers):
+        to = lax.rem(p.n + k, peers)
+        launch(hback_ref.at[to], hret.at[p.n], hssem.at[k], hrsem.at[k], p.z, to)
+    hret[p.n] = hback_ref[p.n]
+    vput[0] = gvec_ref[...]
+    launch(vput.at[0], vgot.at[0], vssem.at[0], vrsem.at[0], p.z, p.sib)
+    plane[NBLOCK] = jnp.zeros((rows, width), f32)
+    blocks = (6, 4, 5, 3, 0, 1, 2)
+    for i in range(NBLOCK + 3):
+        if i < NBLOCK:
+            to_core(blocks[i])
+        if 0 <= i - 1 < NBLOCK:
+            to_first(blocks[i - 1])
+        if 0 <= i - 2 < NBLOCK:
+            to_second(blocks[i - 2])
+        if 0 <= i - 3 < NBLOCK:
+            settle(blocks[i - 3])
+        if i == 1:
+            landed(vgot.at[0], vrsem.at[0])
+            vput[1] = vput[0] + vgot[0]
+            launch(vput.at[1], vgot.at[1], vssem.at[1], vrsem.at[1], p.z, p.xn)
+        if i == 3:
+            landed(vgot.at[1], vrsem.at[1])
+            vput[2] = vput[1] + vgot[1]
+            launch(vput.at[2], vgot.at[2], vssem.at[2], vrsem.at[2], p.z, p.yn)
+        if i == 5:
+            landed(vgot.at[2], vrsem.at[2])
+            vz[p.z] = vput[2] + vgot[2]
+            vput[3] = vput[2] + vgot[2]
+            for k in range(1, depth):
+                to = lax.rem(p.z + k, depth)
+                launch(vput.at[3], vz.at[p.z], vssem.at[2 + k], vrsem.at[2 + k], to, p.n)
+
+    def slot_sum(s):
+        return plane[jnp.minimum(slot_block_ref[s], NBLOCK)]
+
+    def part(target, s):
+        return slot_sum(target * slot_dev + s)
+
+    def pass_on(way):
+        put, got = (put_up, got_up) if way == 0 else (put_down, got_down)
+        source = p.z > 0 if way == 0 else p.z < depth - 1
+        for i in range(depth - 1):
+            target = depth - 1 - i if way == 0 else i
+            test = p.z < target if way == 0 else p.z > target
+            at = p.z + 1 if way == 0 else p.z - 1
+
+            @pl.when(test)
+            def _():
+                for s in range(slot_dev):
+
+                    @pl.when(source)
+                    def _():
+                        landed(got.at[target, s], zrsem.at[way, target, s])
+                        total = part(target, s) + got[target, s].astype(f32)
+                        put[target, s] = total.astype(bf16)
+
+                    @pl.when(jnp.logical_not(source))
+                    def _():
+                        put[target, s] = part(target, s).astype(bf16)
+
+                    remote(
+                        put.at[target, s],
+                        got.at[target, s],
+                        zssem.at[way, target, s],
+                        zrsem.at[way, target, s],
+                        at,
+                        p.n,
+                    ).start()
+
+    @pl.when(p.z < depth // 2)
+    def _():
+        pass_on(0)
+        pass_on(1)
+
+    @pl.when(p.z >= depth // 2)
+    def _():
+        pass_on(1)
+        pass_on(0)
+
+    for k in range(1, peers):
+        landed(hret.at[0], hrsem.at[k])
+    ids = lax.broadcasted_iota(jnp.int32, (nodes, per_peer * peers), 0)
+    pick_t = jnp.where(ids == send_rows_ref[...], 1.0, 0.0).astype(bf16)
+    back = hret[...].astype(f32).reshape(peers, roll, per_peer, width)
+    for t in range(roll):
+        rows_t = back[:, t].reshape(peers * per_peer, width).astype(bf16)
+        ngrad_ref[0, t] = (nbase_ref[t * nodes : (t + 1) * nodes] + dot(pick_t, rows_t)).astype(bf16)
+
+    own = []
+    square = jnp.zeros((8, width), f32)
+    for s in range(slot_dev):
+        mine = slot_sum(p.z * slot_dev + s)
+
+        @pl.when(p.z > 0)
+        def _():
+            landed(got_up.at[p.z, s], zrsem.at[0, p.z, s])
+
+        @pl.when(p.z < depth - 1)
+        def _():
+            landed(got_down.at[p.z, s], zrsem.at[1, p.z, s])
+
+        mine = mine + jnp.where(p.z > 0, got_up[p.z, s].astype(f32), 0.0)
+        mine = mine + jnp.where(p.z < depth - 1, got_down[p.z, s].astype(f32), 0.0)
+        full[s, p.n] = mine.astype(bf16)
+        for copy in gather_start(p, lambda k, n: full.at[k, n], s, (gssem, grsem)):
+            going.append((copy, None))
+        square = square + eights(mine * mine)
+    square = square[:, :128] + square[:, 128:256] + square[:, 256:384] + square[:, 384:]
+    sput[...] = square
+    sgot[p.n] = square
+    for k in range(1, peers):
+        to = lax.rem(p.n + k, peers)
+        launch(sput, sgot.at[p.n], nssem.at[k], nrsem.at[k], p.z, to)
+
+    def collect(buf, sems, finish):
+        for s in range(slot_dev):
+            going.extend((copy, None) for copy in gather_side(p, buf, s, sems))
+        for s in range(slot_dev):
+            going.extend((copy, None) for copy in gather_far(p, buf, s, sems))
+        for s in range(slot_dev):
+            gather_end(p, buf, s, sems)
+            finish(s)
+
+    for k in range(1, peers):
+        landed(sgot.at[0], nrsem.at[k])
+    szput[...] = jnp.sum(sgot[...], axis=0)
+    sz[p.z] = szput[...]
+    for k in range(1, depth):
+        to = lax.rem(p.z + k, depth)
+        launch(szput, sz.at[p.z], nssem.at[peers - 1 + k], nrsem.at[peers - 1 + k], to, p.n)
+
+    rotated = [None] * slot_dev
+
+    def rotate(s):
+        part_left = dot_ta(left_ref[s].astype(bf16), full[s].reshape(width, width))
+        rotated[s] = dot(part_left.astype(bf16), right_ref[s].astype(bf16))
+
+    collect(lambda k, n: full.at[k, n], (gssem, grsem), rotate)
+    for k in range(1, depth):
+        landed(vz.at[0], vrsem.at[2 + k])
+        landed(sz.at[0], nrsem.at[peers - 1 + k])
+    grad_vectors = vz[0] + vz[1] + vz[2] + vz[3]
+    square_sum = jnp.sum(sz[0] + sz[1] + sz[2] + sz[3], keepdims=True).reshape(1, 1)
+    square_sum = square_sum + jnp.sum(grad_vectors * grad_vectors, keepdims=True).reshape(1, 1)
+    grad_norm = jnp.sqrt(square_sum)
+    norm_ref[...] = jnp.broadcast_to(grad_norm, norm_ref.shape)
+    limit = math.sqrt(NBLOCK * width * width + 8 * width)
+    clip = jnp.minimum(1.0, limit / grad_norm)
+
+    def fix(beta, step):
+        return 1.0 - jnp.exp2(math.log2(beta) * jnp.full((1, 1), step, jnp.int32).astype(f32))
+
+    tbuf = lambda k, n: turned.at[k, n]
+    for s in range(slot_dev):
+        step = step_ref[p.z * slot_dev + s]
+        spun = rotated[s] * clip
+        one = beta_first * first_ref[s] + (1.0 - beta_first) * spun
+        two = beta_second * second_ref[s] + (1.0 - beta_second) * spun * spun
+        mone_ref[s] = one
+        mtwo_ref[s] = two
+        direction = adam_direction(one, two, fix(beta_first, step), fix(beta_second, step))
+        turned[s, p.n] = dot_tb(direction.astype(bf16), right_ref[s].astype(bf16)).astype(bf16)
+        for copy in gather_start(p, tbuf, s, (tssem, trsem)):
+            going.append((copy, None))
+
+    step = step_ref[depth * slot_dev]
+    spun = grad_vectors * clip
+    one = beta_first * vfirst_ref[...] + (1.0 - beta_first) * spun
+    two = beta_second * vsecond_ref[...] + (1.0 - beta_second) * spun * spun
+    vstate_ref[0] = vec_ref[...] - rate_vector * adam_direction(
+        one, two, fix(beta_first, step), fix(beta_second, step)
+    )
+    vstate_ref[1] = one
+    vstate_ref[2] = two
+
+    def finish(s):
+        reverted = dot_ta(left_t_ref[s], turned[s].reshape(width, width))
+        new = weight_ref[s] - rate_matrix * (reverted + weight_decay * weight_ref[s])
+        wnew_ref[s] = new
+        wcopy_ref[s] = new.astype(bf16)
+
+    collect(tbuf, (tssem, trsem), finish)
+
+    for copy, _ in going:
+        copy.wait_send()
+    for i in range(depth - 1):
+        for s in range(slot_dev):
+            for test, target, way, put in (
+                (p.z < depth - 1 - i, depth - 1 - i, 0, put_up),
+                (p.z > i, i, 1, put_down),
+            ):
+                sent = remote(
+                    put.at[target, s],
+                    put.at[target, s],
+                    zssem.at[way, target, s],
+                    zrsem.at[way, target, s],
+                    p.z,
+                    p.sib,
+                )
+                pl.when(test)(sent.wait_send)
+
+
+def update(
+    slot_block,
+    step_count,
+    grads,
+    grad_vectors,
+    halo_back,
+    node_base,
+    send_rows,
+    weight_slots,
+    moment_first,
+    moment_second,
+    basis_left,
+    basis_right,
+    left_t,
+    vector_params,
+    vector_first,
+    vector_second,
+    node_shape,
+):
+    depth, peers = 4, 8
+    slot_dev, rows, width = weight_slots.shape
+    vmem = pl.BlockSpec(memory_space=pltpu.VMEM)
+    smem = pl.BlockSpec(memory_space=pltpu.SMEM)
+    shape = jax.ShapeDtypeStruct
+    dma = pltpu.SemaphoreType.DMA
+    own = (slot_dev, rows, width)
+    tile = (8, 128)
+    *results, norm = pl.pallas_call(
+        update_kernel,
+        out_shape=(
+            shape(node_shape, bf16),
+            shape(own, f32),
+            shape(own, f32),
+            shape(own, f32),
+            shape(own, bf16),
+            shape((3, 8, width), f32),
+            shape(tile, f32),
+        ),
+        in_specs=[smem] * 2 + [vmem] * 14,
+        out_specs=(vmem,) * 7,
+        scratch_shapes=[
+            pltpu.VMEM((NBLOCK, peers // 2, 2, rows, width), bf16),
+            pltpu.VMEM((NBLOCK, peers // 2, rows, width), bf16),
+            pltpu.VMEM((NBLOCK, 2, 2, rows, width), bf16),
+            pltpu.VMEM((NBLOCK, 2, rows, width), f32),
+            pltpu.VMEM((NBLOCK, 2, rows, width), bf16),
+            pltpu.VMEM((NBLOCK, rows, width), bf16),
+            pltpu.VMEM((NBLOCK, rows, width), f32),
+            pltpu.VMEM((NBLOCK, rows, width), bf16),
+            pltpu.VMEM((NBLOCK + 1, rows, width), f32),
+            pltpu.VMEM((depth, *own), bf16),
+            pltpu.VMEM((depth, *own), bf16),
+            pltpu.VMEM((depth, *own), bf16),
+            pltpu.VMEM((depth, *own), bf16),
+            pltpu.VMEM((slot_dev, peers, rows, width), bf16),
+            pltpu.VMEM((slot_dev, peers, rows, width), bf16),
+            pltpu.VMEM((peers, halo_back.shape[0] // peers, width), bf16),
+            pltpu.VMEM((4, 8, width), f32),
+            pltpu.VMEM((3, 8, width), f32),
+            pltpu.VMEM((depth, 8, width), f32),
+            pltpu.VMEM(tile, f32),
+            pltpu.VMEM((peers, *tile), f32),
+            pltpu.VMEM(tile, f32),
+            pltpu.VMEM((depth, *tile), f32),
+            dma((3, NBLOCK)),
+            dma((3, NBLOCK)),
+            dma((7, slot_dev)),
+            dma((7, slot_dev)),
+            dma((7, slot_dev)),
+            dma((7, slot_dev)),
+            dma((2, depth, slot_dev)),
+            dma((2, depth, slot_dev)),
+            dma((peers,)),
+            dma((peers,)),
+            dma((6,)),
+            dma((6,)),
+            dma((peers + depth - 1,)),
+            dma((peers + depth - 1,)),
+        ],
+        compiler_params=pltpu.CompilerParams(
+            vmem_limit_bytes=50 << 20, collective_id=1, has_side_effects=True
+        ),
+        name="update",
+    )(
+        slot_block,
+        step_count,
+        grads.reshape(NBLOCK, peers, rows, width),
+        grad_vectors,
+        halo_back.reshape(peers, -1, width),
+        node_base,
+        send_rows,
+        weight_slots,
+        moment_first,
+        moment_second,
+        basis_left,
+        basis_right,
+        left_t,
+        vector_params,
+        vector_first,
+        vector_second,
+    )
+    return *results, norm[0, :1]
+
+
 def local(
     node_state,
     edge_state,
@@ -347,6 +986,42 @@
     halo_rows = send_rows.shape[1]
     peers = lax.axis_size("node")
     per_peer = halo_rows // peers
+    if (lax.axis_size("dp"), peers) == (4, 8):
+        slots, halo, left_t = prepare(weight_slots, node_state, send_rows, basis_left)
+        node_output, edge_output, node_base, edge_gradient, grads, grad_vectors, halo_back = layer(
+            rollout_length,
+            slot_block,
+            node_state,
+            edge_state,
+            node_cotangent,
+            edge_cotangent,
+            edge_sender,
+            edge_receiver,
+            halo,
+            slots,
+            vector_params,
+            per_peer,
+        )
+        node_gradient, *results = update(
+            slot_block,
+            step_count,
+            grads,
+            grad_vectors,
+            halo_back,
+            node_base,
+            send_rows,
+            weight_slots,
+            moment_first,
+            moment_second,
+            basis_left,
+            basis_right,
+            left_t,
+            vector_params,
+            vector_first,
+            vector_second,
+            node_state.shape,
+        )
+        return node_output, edge_output, node_gradient, edge_gradient, *results
     copies = lax.all_gather(weight_slots.astype(bf16), "node", axis=1, tiled=True)
     slots = lax.all_gather(copies, "dp", axis=0, tiled=True)
     back_onehot = (send_rows[0][:, None] == jnp.arange(nodes, dtype=jnp.int32)[None, :]).astype(bf16)

time: 425 us -> 157 us (0.37)
  waiting for transfers between devices: 269 us -> 0 us
  Pallas kernels: 39.9 us -> 140 us
  blocking collectives: 42 us -> 0 us
  matrix products: 23.1 us -> 0 us
  between operations: 18.6 us -> 1.47 us
  other arithmetic: 9.97 us -> 0 us
  starting transfers between devices: 8.24 us -> 0 us
    psum x1 -> x0, waiting for transfers between devices: 121 us -> none  [local(): summed, grad_vectors = lax.psum((grads, grad_vectors), ('dp', 'node'))]
    pallas_call x0 -> x2, Pallas kernels: none -> 99.6 us  [the longest x1 64.4 us: update(): pl.pallas_call(update_kernel, out_shape=(shape(node_shape, bf16), shape(o...]
    all_gather x2 -> x0, waiting for transfers between devices: 98.1 us -> none  [the longest x1 70.6 us: local(): slots = lax.all_gather(copies, 'dp', axis=0, tiled=True)]
    unnamed x5 -> x0, waiting for transfers between devices: 46.9 us -> none
    psum x1 -> x0, blocking collectives: 42 us -> none  [local(): summed, grad_vectors = lax.psum((grads, grad_vectors), ('dp', 'node'))]
    dot_general x7 -> x0, matrix products: 23.1 us -> none  [the longest x1 12.7 us: local(): owned_grads = jnp.einsum('bs,bij->sij', mine, summed, precision=highest)]
    all_to_all x2 -> x0, starting transfers between devices: 8.16 us -> none  [the longest x1 4.6 us: local(): lax.all_to_all(halo_back, 'node', split_axis=0, concat_axis=0, tiled=True)]
    unnamed x40 -> x39, local copies, waits for them, and re-layouts: 5.43 us -> 12.4 us
  transfers between devices with their start and end apart: 6 -> 0, of which waited for: 5 -> 0; matrix products, arithmetic and copies ran while one was open for 9% -> 0% of each run, Pallas kernels for 0% -> 0%
where the time goes in v1:
time: 157 us
  Pallas kernels  140 us (89%)
  local copies, waits for them, and re-layouts  15.5 us (10%)
    pallas_call x1, Pallas kernels, update(): pl.pallas_call(update_kernel, out_shape=(shape(node_shape, bf16), shape(o...  64.4 us
    pallas_call x1, Pallas kernels, layer(): pl.pallas_call(layer_kernel, out_shape=(shape(node_state.shape, bf16), sh...  39.9 us
    pallas_call x1, Pallas kernels, prepare(): pl.pallas_call(prepare_kernel, out_shape=(shape((slot_dev * depth, peers,...  35.2 us
    unnamed x39, local copies, waits for them, and re-layouts  12.4 us

profile of v1, /device:TPU:1, one launch (start us, length us, event | category | flops | bytes accessed | tf_op | source)
XLA Modules:
  0.0 156.5 jit_solution(9527858569209485308)
XLA Ops:
  1.3 1.3 reshape.41.sender_ref
  2.6 1.3 reshape.42.receiver_ref
  3.8 1.1 copy.28.left_ref
  5.0 0.0 copy-start.1
  5.0 1.0 copy-done.1
  6.0 0.0 copy-start.2
  6.0 0.9 copy-done.2
  7.0 0.0 copy-start.13
  7.0 0.7 copy-done.13
  7.6 35.2 %prepare.1 = (bf16[8,8,64,512]{3,2,1,0:T(8,128)(2,1)S(1)}, bf16[8,32,512]{2,1,0:T(8,128)(2,1)S(1)}, bf16[2,8,64,64]{3,2,1,0:T(8,128)(2,1)S(1)}) custom-call(f32[2,64,512]{2,1,0:T(8,128)S(1)} %copy-done.2, bf16[1,4,128,512]{3,2,1,0:T(8,128)(2,1)S(1)} %copy-done.1, s32[1,64]{1,0:T(1,128)S(1)} %copy-done.13, f32[2,512,64]{2,1,0:T(8,128)S(1)} %copy.28.left_ref), custom_call_target="tpu_custom_call" | custom-call | tf_op jit(solution)/shard_map/prepare/pallas_call | solution.py:507
  42.9 0.0 copy-start
  42.9 2.1 %copy-done = bf16[8,8,64,512]{3,2,1,0:T(8,128)(2,1)} copy-done((bf16[8,8,64,512]{3,2,1,0:T(8,128)(2,1)}, bf16[8,8,64,512]{3,2,1,0:T(8,128)(2,1)S(1)}, u32[]{:S(2)}) %copy-start) | copy-done | bytes 4194328
  45.0 0.0 copy-start.7
  45.0 0.7 copy-done.7
  45.7 0.0 copy-start.3
  45.7 0.0 copy-start.4
  45.7 0.0 copy-start.5
  45.7 0.0 copy-start.8
  45.7 0.0 copy-start.9
  45.7 0.0 copy-start.10
  45.7 0.0 copy-start.12
  45.7 0.0 copy-start.14
  45.7 0.0 copy-start.15
  45.7 39.9 %layer.1 = (bf16[1,4,128,512]{3,2,1,0:T(8,128)(2,1)}, bf16[1,4,768,512]{3,2,1,0:T(8,128)(2,1)}, f32[512,512]{1,0:T(8,128)}, bf16[1,4,768,512]{3,2,1,0:T(8,128)(2...) custom-call(s32[1]{0:T(128)S(6)} %copy.36.rollout_ref, s32[8]{0:T(128)} %slot_block_ref.3, ...), custom_call_target="tpu_custom_call" | custom-call | tf_op jit(solution)/shard_map/layer/pallas_call | solution.py:263
  85.7 0.0 copy-done.3
  85.7 0.0 copy-done.4
  85.7 0.0 copy-done.5
  85.7 0.0 copy-done.8
  85.7 0.0 copy-done.9
  85.7 0.0 copy-done.10
  85.7 0.0 copy-done.12
  85.7 0.0 copy-done.14
  85.7 0.0 copy-done.15
  85.8 0.0 copy-start.6
  85.8 0.9 copy-done.6
  86.7 0.0 copy-start.11
  86.7 0.7 copy-done.11
  87.4 64.4 %update.1 = (bf16[1,4,128,512]{3,2,1,0:T(8,128)(2,1)S(1)}, f32[2,64,512]{2,1,0:T(8,128)S(1)}, f32[2,64,512]{2,1,0:T(8,128)S(1)}, f32[2,64,512]{2,1,0:T(8,128)S(1...) custom-call(s32[8]{0:T(128)S(1)} %copy-done.12, s32[9]{0:T(128)S(1)} %copy-done.15, ...), custom_call_target="tpu_custom_call" | custom-call | tf_op jit(solution)/shard_map/update/pallas_call | solution.py:884
  151.8 0.5 slice.3
  152.4 0.8 copy.37
  153.1 0.7 copy.38
  153.8 0.7 copy.39
  154.6 0.7 copy.40
  155.3 0.7 copy.41
  155.9 0.6 copy.42
Async XLA Ops:
  5.0 1.0 copy-start.1
  6.0 0.9 copy-start.2
  7.0 0.7 copy-start.13
  42.9 2.1 %copy-start = (bf16[8,8,64,512]{3,2,1,0:T(8,128)(2,1)}, bf16[8,8,64,512]{3,2,1,0:T(8,128)(2,1)S(1)}, u32[]{:S(2)}) copy-start(bf16[8,8,64,512]{3,2,1,0:T(8,128)(2,1)S(1)} %get-tuple-element.28) | copy-start | bytes 12582916
  45.0 0.7 copy-start.7
  45.7 40.0 %copy-start.3 = (f32[2,64,512]{2,1,0:T(8,128)S(1)}, f32[2,64,512]{2,1,0:T(8,128)}, u32[]{:S(2)}) copy-start(f32[2,64,512]{2,1,0:T(8,128)} %weight_ref.3) | copy-start | bytes 786436
  45.7 40.0 %copy-start.4 = (f32[2,64,512]{2,1,0:T(8,128)S(1)}, f32[2,64,512]{2,1,0:T(8,128)}, u32[]{:S(2)}) copy-start(f32[2,64,512]{2,1,0:T(8,128)} %first_ref.1) | copy-start | bytes 786436
  45.7 40.0 %copy-start.5 = (f32[2,64,512]{2,1,0:T(8,128)S(1)}, f32[2,64,512]{2,1,0:T(8,128)}, u32[]{:S(2)}) copy-start(f32[2,64,512]{2,1,0:T(8,128)} %second_ref.1) | copy-start | bytes 786436
  45.7 40.0 %copy-start.8 = (f32[8,512]{1,0:T(8,128)S(1)}, f32[8,512]{1,0:T(8,128)}, u32[]{:S(2)}) copy-start(f32[8,512]{1,0:T(8,128)} %vec_ref.3) | copy-start | bytes 49156
  45.7 40.0 %copy-start.9 = (f32[8,512]{1,0:T(8,128)S(1)}, f32[8,512]{1,0:T(8,128)}, u32[]{:S(2)}) copy-start(f32[8,512]{1,0:T(8,128)} %vfirst_ref.1) | copy-start | bytes 49156
  45.7 40.0 %copy-start.10 = (f32[8,512]{1,0:T(8,128)S(1)}, f32[8,512]{1,0:T(8,128)}, u32[]{:S(2)}) copy-start(f32[8,512]{1,0:T(8,128)} %vsecond_ref.1) | copy-start | bytes 49156
  45.7 40.0 %copy-start.12 = (s32[8]{0:T(128)S(1)}, s32[8]{0:T(128)}, u32[]{:S(2)}) copy-start(s32[8]{0:T(128)} %slot_block_ref.3) | copy-start | bytes 100
  45.7 40.0 %copy-start.14 = (s32[1,64]{1,0:T(1,128)S(1)}, s32[1,64]{1,0:T(1,128)}, u32[]{:S(2)}) copy-start(s32[1,64]{1,0:T(1,128)} %send_rows_ref.3) | copy-start | bytes 772
  45.7 40.0 %copy-start.15 = (s32[9]{0:T(128)S(1)}, s32[9]{0:T(128)}, u32[]{:S(2)}) copy-start(s32[9]{0:T(128)} %step_ref.1) | copy-start | bytes 112
  85.8 1.0 copy-start.6
  86.7 0.7 copy-start.11

commit v2 on v0

--- a/solution.py
+++ b/solution.py
@@ -319,6 +319,823 @@
     return moment_one / fix_one / (jnp.sqrt(moment_two / fix_two) + adam_epsilon)
 
 
+MESH = pl.DeviceIdType.MESH
+
+
+class Place:
+    def __init__(self):
+        self.z = lax.axis_index("dp")
+        self.n = lax.axis_index("node")
+        self.c = lax.rem(self.n, 2)
+        self.x = lax.rem(self.n // 2, 2)
+        self.y = self.n // 4
+        self.xn = self.n + 2 - 4 * self.x
+        self.yn = self.n + 4 - 8 * self.y
+        self.sib = self.n + 1 - 2 * self.c
+        self.diag = self.xn + 4 - 8 * self.y
+
+
+def remote(src, dst, send, recv, z, n):
+    return pltpu.make_async_remote_copy(
+        src_ref=src, dst_ref=dst, send_sem=send, recv_sem=recv, device_id=(z, n), device_id_type=MESH
+    )
+
+
+def greet_start(p, depth, peers):
+    barrier = pltpu.get_barrier_semaphore()
+    for k in range(1, peers):
+        to = lax.rem(p.n + k, peers)
+        pl.semaphore_signal(barrier, inc=1, device_id=(p.z, to), device_id_type=MESH)
+    for k in range(1, depth):
+        to = lax.rem(p.z + k, depth)
+        pl.semaphore_signal(barrier, inc=1, device_id=(to, p.n), device_id_type=MESH)
+
+
+def greet_end(depth, peers):
+    pl.semaphore_wait(pltpu.get_barrier_semaphore(), peers + depth - 2)
+
+
+ORDER = ((0, 1, 2, 3), (1, 0, 2, 3), (2, 3, 1, 0), (3, 2, 1, 0))
+
+
+def gather_start(p, buf, k, sems):
+    send, recv = sems
+    own = buf(k, p.n)
+    copies = []
+    for i, to in ((0, p.xn), (1, p.yn), (3, p.sib)):
+        copies.append(remote(own, own, send.at[i, k], recv.at[i, k], p.z, to))
+        copies[-1].start()
+    return copies
+
+
+def gather_side(p, buf, k, sems):
+    send, recv = sems
+    copies = []
+    for i, owner in ((0, p.xn), (1, p.yn)):
+        got = buf(k, owner)
+        remote(got, got, send.at[i, k], recv.at[i, k], p.z, owner).wait_recv()
+        on = remote(got, got, send.at[4 + i, k], recv.at[4 + i, k], p.z, p.sib)
+        on.start()
+        copies.append(on)
+        over = remote(got, got, send.at[2, k], recv.at[2, k], p.z, p.yn if i == 0 else p.xn)
+        pl.when(p.c == i)(over.start)
+    copies.append(over)
+    return copies
+
+
+def gather_far(p, buf, k, sems):
+    send, recv = sems
+    got = buf(k, p.diag)
+    remote(got, got, send.at[2, k], recv.at[2, k], p.z, p.xn).wait_recv()
+    on = remote(got, got, send.at[6, k], recv.at[6, k], p.z, p.sib)
+    on.start()
+    return [on]
+
+
+def gather_end(p, buf, k, sems):
+    send, recv = sems
+    for i in (3, 4, 5, 6):
+        got = buf(k, p.sib)
+        remote(got, got, send.at[i, k], recv.at[i, k], p.z, p.sib).wait_recv()
+
+
+class Step:
+    def __init__(self, **refs):
+        self.__dict__.update(refs)
+
+
+def step_kernel(names, *refs):
+    k = Step(**dict(zip(names, refs, strict=True)))
+    p = Place()
+    depth, peers = 4, 8
+    roll, nodes, width = k.node_v.shape
+    edges = k.edge_v.shape[1]
+    slot_dev, rows = k.weight_v.shape[:2]
+    per_peer = k.halo.shape[1] // roll
+    halo = peers * per_peer
+    known = nodes + halo
+    padded = k.table.shape[1]
+    chunk = 384
+    pieces = edges // chunk
+    going = []
+    leaving = []
+
+    def launch(src, dst, send, recv, z, n):
+        copy = remote(src, dst, send, recv, z, n)
+        copy.start()
+        going.append((copy, None))
+
+    def landed(dst, recv):
+        remote(dst, dst, recv, recv, p.z, p.sib).wait_recv()
+
+    def leave(src, dst, i):
+        copy = pltpu.make_async_copy(src, dst, k.out_sem.at[i])
+        copy.start()
+        leaving.append(copy)
+
+    loads = []
+    for i, (src, dst) in enumerate(
+        (
+            (k.weight_hbm, k.weight_v),
+            (k.node_hbm.at[0], k.node_v),
+            (k.left_hbm, k.grad.at[2, :slot_dev]),
+            (k.right_hbm, k.grad.at[:slot_dev]),
+            (k.edge_hbm.at[0], k.edge_v),
+            (k.ncot_hbm.at[0], k.ncot_v),
+            (k.ecot_hbm.at[0], k.ecot_v),
+            (k.first_hbm, k.first_v),
+            (k.second_hbm, k.second_v),
+        )
+    ):
+        loads.append(pltpu.make_async_copy(src, dst, k.in_sem.at[i]))
+        loads[-1].start()
+    greet_start(p, depth, peers)
+
+    def buf(z, n):
+        return k.slots.at[pl.ds(slot_dev * z, slot_dev), n]
+
+    wsems = (k.w_send, k.w_recv)
+    order = []
+
+    def arrive(j):
+        z_of = 0
+        for z in range(depth):
+            z_of = z_of + jnp.where(p.z == z, ORDER[z][j], 0)
+        order.append(z_of)
+        piece = buf(z_of, p.n)
+        if j:
+            remote(piece, piece, k.wz_send.at[0, z_of], k.wz_recv.at[z_of], p.z, p.n).wait_recv()
+        for i, test, to in (
+            (0, (z_of <= p.z) & (p.z < depth - 1), p.z + 1),
+            (1, (z_of >= p.z) & (p.z > 0), p.z - 1),
+        ):
+            copy = remote(piece, piece, k.wz_send.at[i, z_of], k.wz_recv.at[z_of], to, p.n)
+            pl.when(test)(copy.start)
+            going.append((copy, test))
+        going.extend((copy, None) for copy in gather_start(p, buf, z_of, wsems))
+
+    def side(j):
+        going.extend((copy, None) for copy in gather_side(p, buf, order[j], wsems))
+
+    def far(j):
+        going.extend((copy, None) for copy in gather_far(p, buf, order[j], wsems))
+
+    loads[0].wait()
+    k.slots[pl.ds(slot_dev * p.z, slot_dev), p.n] = k.weight_v[...].astype(bf16)
+    greet_end(depth, peers)
+    arrive(0)
+    loads[1].wait()
+    node_ids = lax.broadcasted_iota(jnp.int32, (nodes, halo), 0)
+    pick_t = jnp.where(node_ids == k.rows_ref[...], 1.0, 0.0).astype(bf16)
+    for t in range(roll):
+        k.spread[:, t] = dot(pick_t.T, k.node_v[t]).reshape(peers, per_peer, width)
+    k.hput[...] = k.spread[...].reshape(peers, roll * per_peer, width).astype(bf16)
+    k.halo[p.n] = k.hput[p.n]
+    hsent = []
+    for i in range(1, peers):
+        to = lax.rem(p.n + i, peers)
+        hsent.append(remote(k.hput.at[to], k.halo.at[p.n], k.h_send.at[0, i], k.h_recv.at[0, i], p.z, to))
+        hsent[-1].start()
+    arrive(1)
+    side(0)
+    loads[2].wait()
+    for s in range(slot_dev):
+        k.left_b[s] = k.grad[2, s].astype(bf16)
+        for m in range(peers):
+            k.lput[s, m] = k.grad[2, s, :, m * rows : (m + 1) * rows].astype(bf16)
+    k.lgot[:, p.n] = k.lput[:, p.n]
+    for i in range(1, peers):
+        to = lax.rem(p.n + i, peers)
+        launch(k.lput.at[:, to], k.lgot.at[:, p.n], k.l_send.at[i], k.l_recv.at[i], p.z, to)
+    arrive(2)
+    side(1)
+    far(0)
+    ids = lax.broadcasted_iota(jnp.int32, (padded, edges), 0)
+    onehot = (ids == k.sender_ref[...].reshape(1, edges)) | (
+        ids == k.receiver_ref[...].reshape(1, edges) + known
+    )
+    onehot = jnp.where(onehot, 1.0, 0.0).astype(f32)
+    k.gather_t[...] = onehot.astype(bf16)
+    arrive(3)
+    side(2)
+    far(1)
+    k.gather[...] = onehot.T.astype(bf16)
+    k.table[:, known + nodes :] = jnp.zeros((roll, padded - known - nodes, width), bf16)
+    k.acc[...] = jnp.zeros_like(k.acc)
+    side(3)
+    far(2)
+    loads[3].wait()
+    for s in range(slot_dev):
+        k.right_b[s] = k.grad[s].reshape(width, width).astype(bf16)
+    far(3)
+    for copy in hsent:
+        copy.wait_send()
+    for i in range(1, peers):
+        landed(k.halo.at[0], k.h_recv.at[0, i])
+        landed(k.lgot.at[:, 0], k.l_recv.at[i])
+    for j in range(depth):
+        gather_end(p, buf, order[j], wsems)
+
+    slot_of = []
+    for b in range(NBLOCK):
+        found = 0
+        for s in range(depth * slot_dev):
+            found = jnp.where(k.slot_block_ref[s] == b, s, found)
+        slot_of.append(found)
+
+    def weight(b):
+        return k.slots[slot_of[b]].reshape(width, width)
+
+    rollout = k.rollout_ref[0]
+    vec = k.vec_ref
+
+    def live(t):
+        return jnp.where(t < rollout, 1.0, 0.0).astype(f32)
+
+    def flat_nodes():
+        return k.node_v[...].reshape(roll * nodes, width)
+
+    own_sent = dot(flat_nodes(), weight(1))
+    own_recv = dot(flat_nodes(), weight(2))
+    halo_flat = k.halo[...].reshape(roll * halo, width)
+    halo_sent = dot(halo_flat, weight(1)).reshape(peers, roll, per_peer, width)
+    for t in range(roll):
+        k.table[t, :nodes] = own_sent[t * nodes : (t + 1) * nodes].astype(bf16)
+        k.table[t, nodes:known] = halo_sent[:, t].reshape(halo, width).astype(bf16)
+        k.table[t, known : known + nodes] = own_recv[t * nodes : (t + 1) * nodes].astype(bf16)
+    loads[4].wait()
+
+    def edge_out(t):
+        return pltpu.make_async_copy(k.eout_v.at[t % 2], k.eout_hbm.at[0, t], k.e_sem.at[t])
+
+    def forward(t, carry):
+        lv = live(t)
+        slot = t % 2
+
+        @pl.when(t >= 2)
+        def _():
+            edge_out(t - 2).wait()
+
+        total = jnp.zeros((nodes, width), f32)
+        for c in range(pieces):
+            at = pl.ds(c * chunk, chunk)
+            edge = k.edge_v[t, at]
+            z = dot(edge, weight(0)) + dot(k.gather[at], k.table[t]) + vec[0:1]
+            hidden, slope, normed, inverse = branch_forward(z, weight(3), vec[1:2])
+            k.hidden_v[t, at] = hidden
+            k.slope_v[t, at] = slope.astype(bf16)
+            k.normed_v[t, at] = normed.astype(bf16)
+            k.inv_v[t, at] = inverse
+            new = edge.astype(f32) + (normed * vec[2:3] + vec[3:4])
+            k.eout_v[slot, at] = (new * lv).astype(bf16)
+            total += dot(k.gather_t[known : known + nodes, at], new.astype(bf16))
+        k.summed_v[pl.ds(t * nodes, nodes)] = total.astype(bf16)
+        edge_out(t).start()
+        return carry
+
+    lax.fori_loop(0, roll, forward, 0)
+
+    on_f = jnp.where(p.c == 0, p.x, p.y)
+    on_g = jnp.where(p.c == 0, p.y, p.x)
+    to_f = jnp.where(p.c == 0, p.xn, p.yn)
+    to_g = jnp.where(p.c == 0, p.yn, p.xn)
+
+    def spot(f, g):
+        return jnp.where(p.c == 0, g * 2 + f, f * 2 + g)
+
+    def hop(stage, b):
+        put, got, to = (
+            (k.cast, k.got_core, p.sib),
+            (k.put_one, k.got_one, to_f),
+            (k.put_two, k.got_two, to_g),
+        )[stage]
+        at = stage * NBLOCK + b
+        return remote(put.at[b], got.at[b], k.r_send.at[at], k.r_recv.at[at], p.z, to)
+
+    def to_core(b):
+        for i in range(peers // 2):
+            k.cast[b, i] = k.grad[b, 2 * i + 1 - p.c].astype(bf16)
+        hop(0, b).start()
+
+    def to_first(b):
+        hop(0, b).wait_recv()
+        for g in range(2):
+            at = spot(1 - on_f, g)
+            k.put_one[b, g] = (k.grad[b, 2 * at + p.c] + k.got_core[b, at].astype(f32)).astype(bf16)
+        hop(1, b).start()
+        for g in range(2):
+            at = spot(on_f, g)
+            k.grad[b, 2 * at + p.c] = k.grad[b, 2 * at + p.c] + k.got_core[b, at].astype(f32)
+
+    def to_second(b):
+        hop(1, b).wait_recv()
+        at = spot(on_f, 1 - on_g)
+        total = k.grad[b, 2 * at + p.c] + k.got_one[b, 1 - on_g].astype(f32)
+        k.put_two[b] = total.astype(bf16)
+        hop(2, b).start()
+        k.grad[b, p.n] = k.grad[b, p.n] + k.got_one[b, on_g].astype(f32)
+
+    def settle(b):
+        hop(2, b).wait_recv()
+        k.grad[b, p.n] = k.grad[b, p.n] + k.got_two[b].astype(f32)
+
+    def put_grad(b, value):
+        k.grad[b] = value.reshape(peers, rows, width)
+
+    summed = k.summed_v[...]
+    z = dot(flat_nodes(), weight(4)) + dot(summed, weight(5)) + vec[4:5]
+    hidden, slope, normed, inverse = branch_forward(z, weight(6), vec[5:6])
+    row_t = lax.broadcasted_iota(jnp.int32, (roll * nodes, 1), 0) // nodes
+    row_live = jnp.where(row_t < rollout, 1.0, 0.0).astype(f32)
+    new = flat_nodes().astype(f32) + (normed * vec[6:7] + vec[7:8])
+    k.nout_v[...] = (new * row_live).astype(bf16).reshape(roll, nodes, width)
+    leave(k.nout_v, k.nout_hbm.at[0], 0)
+    loads[5].wait()
+    d_new = k.ncot_v[...].reshape(roll * nodes, width).astype(f32) * row_live
+    k.acc[6] = eights(d_new * normed)
+    k.acc[7] = eights(d_new)
+    d_after = norm_backward(d_new, normed, inverse, vec[6:7])
+    k.acc[5] = eights(d_after.astype(f32))
+    put_grad(6, dot_ta(hidden, d_after))
+    to_core(6)
+    d_before = (dot_tb(d_after, weight(6)) * slope).astype(bf16)
+    k.acc[4] = eights(d_before.astype(f32))
+    put_grad(4, dot_ta(flat_nodes(), d_before))
+    to_core(4)
+    put_grad(5, dot_ta(summed, d_before))
+    to_core(5)
+    k.summed_v[...] = dot_tb(d_before, weight(5)).astype(bf16)
+    k.nbase_v[...] = d_new + dot_tb(d_before, weight(4))
+    k.grad[0] = jnp.zeros((peers, rows, width), f32)
+    k.grad[3] = jnp.zeros((peers, rows, width), f32)
+    loads[6].wait()
+
+    def backward(t, carry):
+        lv = live(t)
+        for c in range(pieces):
+            at = pl.ds(c * chunk, chunk)
+            d_new = k.ecot_v[t, at].astype(f32) * lv + dot(
+                k.gather[at, known : known + nodes], k.summed_v[pl.ds(t * nodes, nodes)]
+            )
+            k.ecot_v[t, at] = d_new.astype(bf16)
+            normed = k.normed_v[t, at].astype(f32)
+            k.acc[2] += eights(d_new * normed)
+            k.acc[3] += eights(d_new)
+            d_after = norm_backward(d_new, normed, k.inv_v[t, at], vec[2:3])
+            k.acc[1] += eights(d_after.astype(f32))
+            k.normed_v[t, at] = d_after
+            d_before = (dot_tb(d_after, weight(3)) * k.slope_v[t, at].astype(f32)).astype(bf16)
+            k.acc[0] += eights(d_before.astype(f32))
+            k.slope_v[t, at] = d_before
+        k.grad[3] += dot_ta(k.hidden_v[t], k.normed_v[t]).reshape(peers, rows, width)
+        k.grad[0] += dot_ta(k.edge_v[t], k.slope_v[t]).reshape(peers, rows, width)
+        scattered = dot(k.gather_t[...], k.slope_v[t])
+        k.sc_own[pl.ds(t * nodes, nodes)] = scattered[:nodes].astype(bf16)
+        k.sc_recv[pl.ds(t * nodes, nodes)] = scattered[known : known + nodes].astype(bf16)
+        k.spread[:, t] = scattered[nodes:known].reshape(peers, per_peer, width)
+        for step, work in enumerate((to_first, to_second, settle)):
+
+            @pl.when(t == step)
+            def _():
+                def one(b, carry):
+                    work(b)
+                    return carry
+
+                lax.fori_loop(4, NBLOCK, one, 0)
+
+        return carry
+
+    lax.fori_loop(0, roll, backward, 0)
+
+    to_core(3)
+    to_core(0)
+    k.hput[...] = k.spread[...].reshape(peers, roll * per_peer, width).astype(bf16)
+    put_grad(1, dot_ta(flat_nodes(), k.sc_own[...]) + dot_ta(halo_flat, k.hput[...].reshape(roll * halo, width)))
+    to_core(1)
+    put_grad(2, dot_ta(flat_nodes(), k.sc_recv[...]))
+    to_core(2)
+    k.vput[0] = jnp.sum(k.acc[...], axis=1)
+    launch(k.vput.at[0], k.vgot.at[0], k.v_send.at[0], k.v_recv.at[0], p.z, p.sib)
+    for i in range(1, peers):
+        to = lax.rem(p.n + i, peers)
+        launch(k.hput.at[to], k.hret.at[p.n], k.h_send.at[1, i], k.h_recv.at[1, i], p.z, to)
+    k.hret[p.n] = k.hput[p.n]
+    to_first(3)
+    to_first(0)
+
+    def edge_gradient(t):
+        for c in range(pieces):
+            at = pl.ds(c * chunk, chunk)
+            grown = k.ecot_v[t, at].astype(f32) + dot_tb(k.slope_v[t, at], weight(0))
+            k.ecot_v[t, at] = grown.astype(bf16)
+        leave(k.ecot_v.at[t], k.egrad_hbm.at[0, t], 2 + t)
+
+    edge_gradient(0)
+    to_first(1)
+    to_first(2)
+    to_second(3)
+    to_second(0)
+    landed(k.vgot.at[0], k.v_recv.at[0])
+    k.vput[1] = k.vput[0] + k.vgot[0]
+    launch(k.vput.at[1], k.vgot.at[1], k.v_send.at[1], k.v_recv.at[1], p.z, p.xn)
+    edge_gradient(1)
+    to_second(1)
+    to_second(2)
+    settle(3)
+    settle(0)
+    landed(k.vgot.at[1], k.v_recv.at[1])
+    k.vput[2] = k.vput[1] + k.vgot[1]
+    launch(k.vput.at[2], k.vgot.at[2], k.v_send.at[2], k.v_recv.at[2], p.z, p.yn)
+    edge_gradient(2)
+    settle(1)
+    settle(2)
+
+    def part(target, s):
+        b = k.slot_block_ref[target * slot_dev + s]
+        held = k.grad[jnp.minimum(b, NBLOCK - 1), p.n]
+        return jnp.where(b < NBLOCK, held, 0.0)
+
+    def pass_on(way):
+        put, got = (k.put_up, k.got_up) if way == 0 else (k.put_down, k.got_down)
+        source = p.z > 0 if way == 0 else p.z < depth - 1
+        for i in range(depth - 1):
+            target = depth - 1 - i if way == 0 else i
+            test = p.z < target if way == 0 else p.z > target
+            at = p.z + 1 if way == 0 else p.z - 1
+
+            @pl.when(test)
+            def _():
+                for s in range(slot_dev):
+
+                    @pl.when(source)
+                    def _():
+                        landed(got.at[target, s], k.z_recv.at[way, target, s])
+                        total = part(target, s) + got[target, s].astype(f32)
+                        put[target, s] = total.astype(bf16)
+
+                    @pl.when(jnp.logical_not(source))
+                    def _():
+                        put[target, s] = part(target, s).astype(bf16)
+
+                    remote(
+                        put.at[target, s],
+                        got.at[target, s],
+                        k.z_send.at[way, target, s],
+                        k.z_recv.at[way, target, s],
+                        at,
+                        p.n,
+                    ).start()
+
+    @pl.when(p.z < depth // 2)
+    def _():
+        pass_on(0)
+        pass_on(1)
+
+    @pl.when(p.z >= depth // 2)
+    def _():
+        pass_on(1)
+        pass_on(0)
+
+    landed(k.vgot.at[2], k.v_recv.at[2])
+    k.vput[3] = k.vput[2] + k.vgot[2]
+    k.vz[p.z] = k.vput[3]
+    for i in range(1, depth):
+        to = lax.rem(p.z + i, depth)
+        launch(k.vput.at[3], k.vz.at[p.z], k.v_send.at[2 + i], k.v_recv.at[2 + i], to, p.n)
+    edge_gradient(3)
+    for i in range(1, peers):
+        landed(k.hret.at[0], k.h_recv.at[1, i])
+    back = k.hret[...].astype(f32).reshape(peers, roll, per_peer, width)
+    for t in range(roll):
+        at = pl.ds(t * nodes, nodes)
+        rows_t = back[:, t].reshape(halo, width).astype(bf16)
+        k.sc_own[at] = (k.sc_own[at].astype(f32) + dot(pick_t, rows_t)).astype(bf16)
+    grown = k.nbase_v[...] + dot_tb(k.sc_own[...], weight(1)) + dot_tb(k.sc_recv[...], weight(2))
+    k.ngrad_v[...] = grown.astype(bf16).reshape(roll, nodes, width)
+    leave(k.ngrad_v, k.ngrad_hbm.at[0], 1)
+
+    square = jnp.zeros((8, width), f32)
+    gsems = (k.g_send, k.g_recv)
+    gbuf = lambda s, n: k.full.at[s, n]
+    for s in range(slot_dev):
+
+        @pl.when(p.z > 0)
+        def _():
+            landed(k.got_up.at[p.z, s], k.z_recv.at[0, p.z, s])
+
+        @pl.when(p.z < depth - 1)
+        def _():
+            landed(k.got_down.at[p.z, s], k.z_recv.at[1, p.z, s])
+
+        mine = part(p.z, s) + jnp.where(p.z > 0, k.got_up[p.z, s].astype(f32), 0.0)
+        mine = mine + jnp.where(p.z < depth - 1, k.got_down[p.z, s].astype(f32), 0.0)
+        k.full[s, p.n] = mine.astype(bf16)
+        for copy in gather_start(p, gbuf, s, gsems):
+            going.append((copy, None))
+        square = square + eights(mine * mine)
+    square = square[:, :128] + square[:, 128:256] + square[:, 256:384] + square[:, 384:]
+    k.sput[...] = square
+    k.sgot[p.n] = square
+    for i in range(1, peers):
+        to = lax.rem(p.n + i, peers)
+        launch(k.sput, k.sgot.at[p.n], k.n_send.at[i], k.n_recv.at[i], p.z, to)
+
+    def collect(buffer, sems, finish):
+        for s in range(slot_dev):
+            going.extend((copy, None) for copy in gather_side(p, buffer, s, sems))
+        for s in range(slot_dev):
+            going.extend((copy, None) for copy in gather_far(p, buffer, s, sems))
+        for s in range(slot_dev):
+            gather_end(p, buffer, s, sems)
+            finish(s)
+
+    for i in range(1, peers):
+        landed(k.sgot.at[0], k.n_recv.at[i])
+    k.szput[...] = jnp.sum(k.sgot[...], axis=0)
+    k.sz[p.z] = k.szput[...]
+    for i in range(1, depth):
+        to = lax.rem(p.z + i, depth)
+        launch(k.szput, k.sz.at[p.z], k.n_send.at[peers - 1 + i], k.n_recv.at[peers - 1 + i], to, p.n)
+
+    rotated = [None] * slot_dev
+
+    def rotate(s):
+        part_left = dot(k.left_b[s], k.full[s].reshape(width, width))
+        rotated[s] = dot(part_left.astype(bf16), k.right_b[s])
+
+    collect(gbuf, gsems, rotate)
+    for i in range(1, depth):
+        landed(k.vz.at[0], k.v_recv.at[2 + i])
+        landed(k.sz.at[0], k.n_recv.at[peers - 1 + i])
+    grad_vectors = k.vz[0] + k.vz[1] + k.vz[2] + k.vz[3]
+    square_sum = jnp.sum(k.sz[0] + k.sz[1] + k.sz[2] + k.sz[3], keepdims=True).reshape(1, 1)
+    square_sum = square_sum + jnp.sum(grad_vectors * grad_vectors, keepdims=True).reshape(1, 1)
+    grad_norm = jnp.sqrt(square_sum)
+    k.norm_v[...] = jnp.broadcast_to(grad_norm, k.norm_v.shape)
+    leave(k.norm_v, k.norm_hbm, 2 + roll)
+    limit = math.sqrt(NBLOCK * width * width + 8 * width)
+    clip = jnp.minimum(1.0, limit / grad_norm)
+
+    def fix(beta, step):
+        return 1.0 - jnp.exp2(math.log2(beta) * jnp.full((1, 1), step, jnp.int32).astype(f32))
+
+    tsems = (k.t_send, k.t_recv)
+    tbuf = lambda s, n: k.turned.at[s, n]
+    loads[7].wait()
+    loads[8].wait()
+    for s in range(slot_dev):
+        step = k.step_ref[p.z * slot_dev + s]
+        spun = rotated[s] * clip
+        one = beta_first * k.first_v[s] + (1.0 - beta_first) * spun
+        two = beta_second * k.second_v[s] + (1.0 - beta_second) * spun * spun
+        k.first_v[s] = one
+        k.second_v[s] = two
+        direction = adam_direction(one, two, fix(beta_first, step), fix(beta_second, step))
+        k.turned[s, p.n] = dot_tb(direction.astype(bf16), k.right_b[s]).astype(bf16)
+        for copy in gather_start(p, tbuf, s, tsems):
+            going.append((copy, None))
+    leave(k.first_v, k.first_out, 3 + roll)
+    leave(k.second_v, k.second_out, 4 + roll)
+
+    step = k.step_ref[depth * slot_dev]
+    spun = grad_vectors * clip
+    one = beta_first * k.vfirst_ref[...] + (1.0 - beta_first) * spun
+    two = beta_second * k.vsecond_ref[...] + (1.0 - beta_second) * spun * spun
+    k.vstate_v[0] = vec[...] - rate_vector * adam_direction(
+        one, two, fix(beta_first, step), fix(beta_second, step)
+    )
+    k.vstate_v[1] = one
+    k.vstate_v[2] = two
+    leave(k.vstate_v, k.vstate_hbm, 5 + roll)
+
+    def finish(s):
+        left_back = k.lgot[s].reshape(width, rows)
+        reverted = dot_ta(left_back, k.turned[s].reshape(width, width))
+        new = k.weight_v[s] - rate_matrix * (reverted + weight_decay * k.weight_v[s])
+        k.wnew_v[s] = new
+        k.wcopy_v[s] = new.astype(bf16)
+        leave(k.wnew_v.at[s], k.wnew_hbm.at[s], 6 + roll + s)
+        leave(k.wcopy_v.at[s], k.wcopy_hbm.at[s], 6 + roll + slot_dev + s)
+
+    collect(tbuf, tsems, finish)
+
+    for copy, test in going:
+        if test is None:
+            copy.wait_send()
+        else:
+            pl.when(test)(copy.wait_send)
+    for b in range(NBLOCK):
+        for stage in range(3):
+            hop(stage, b).wait_send()
+    for i in range(depth - 1):
+        for s in range(slot_dev):
+            for test, target, way, put in (
+                (p.z < depth - 1 - i, depth - 1 - i, 0, k.put_up),
+                (p.z > i, i, 1, k.put_down),
+            ):
+                sent = remote(
+                    put.at[target, s],
+                    put.at[target, s],
+                    k.z_send.at[way, target, s],
+                    k.z_recv.at[way, target, s],
+                    p.z,
+                    p.sib,
+                )
+                pl.when(test)(sent.wait_send)
+    for t in (roll - 2, roll - 1):
+        edge_out(t).wait()
+    for copy in leaving:
+        copy.wait()
+
+
+def copy_kernel(*refs):
+    count = 9
+    sources, norm, targets, norm_out = refs[:count], refs[count], refs[count + 1 : -count - 3], refs[-count - 3]
+    stage, in_sem, out_sem = refs[-count - 2 : -2], refs[-2], refs[-1]
+    first, second = [], []
+    for i in range(count):
+        first.append(pltpu.make_async_copy(sources[i], stage[i], in_sem.at[i]))
+        second.append(pltpu.make_async_copy(stage[i], targets[i], out_sem.at[i]))
+        first[-1].start()
+    norm_out[0] = norm[0, 0]
+    for i in range(count):
+        first[i].wait()
+        second[i].start()
+    for copy in second:
+        copy.wait()
+
+
+def whole_step(
+    node_state,
+    edge_state,
+    node_cotangent,
+    edge_cotangent,
+    send_rows,
+    edge_sender,
+    edge_receiver,
+    rollout_length,
+    slot_block,
+    step_count,
+    weight_slots,
+    moment_first,
+    moment_second,
+    basis_left,
+    basis_right,
+    vector_params,
+    vector_first,
+    vector_second,
+):
+    depth, peers = 4, 8
+    _, roll, nodes, width = node_state.shape
+    edges = edge_state.shape[2]
+    slot_dev, rows = weight_slots.shape[:2]
+    halo = send_rows.shape[1]
+    per_peer = halo // peers
+    padded = -(-(2 * nodes + halo) // 128) * 128
+    own = (slot_dev, rows, width)
+    tile = (8, 128)
+    hbm = pl.BlockSpec(memory_space=pl.ANY)
+    vmem = pl.BlockSpec(memory_space=pltpu.VMEM)
+    smem = pl.BlockSpec(memory_space=pltpu.SMEM)
+    shape = jax.ShapeDtypeStruct
+    dma = pltpu.SemaphoreType.DMA
+    ins = dict(
+        rollout_ref=(rollout_length, smem),
+        slot_block_ref=(slot_block, smem),
+        step_ref=(step_count, smem),
+        node_hbm=(node_state, hbm),
+        edge_hbm=(edge_state, hbm),
+        ncot_hbm=(node_cotangent, hbm),
+        ecot_hbm=(edge_cotangent, hbm),
+        rows_ref=(send_rows, vmem),
+        sender_ref=(edge_sender, vmem),
+        receiver_ref=(edge_receiver, vmem),
+        weight_hbm=(weight_slots, hbm),
+        first_hbm=(moment_first, hbm),
+        second_hbm=(moment_second, hbm),
+        left_hbm=(jnp.swapaxes(basis_left, 1, 2), hbm),
+        right_hbm=(basis_right.reshape(slot_dev, peers, rows, width), hbm),
+        vec_ref=(vector_params, vmem),
+        vfirst_ref=(vector_first, vmem),
+        vsecond_ref=(vector_second, vmem),
+    )
+    outs = dict(
+        nout_hbm=shape(node_state.shape, bf16),
+        eout_hbm=shape(edge_state.shape, bf16),
+        ngrad_hbm=shape(node_state.shape, bf16),
+        egrad_hbm=shape(edge_state.shape, bf16),
+        first_out=shape(own, f32),
+        second_out=shape(own, f32),
+        wnew_hbm=shape(own, f32),
+        wcopy_hbm=shape(own, bf16),
+        vstate_hbm=shape((3, 8, width), f32),
+        norm_hbm=shape(tile, f32),
+    )
+    v = pltpu.VMEM
+    scratch = dict(
+        weight_v=v(own, f32),
+        node_v=v((roll, nodes, width), bf16),
+        edge_v=v((roll, edges, width), bf16),
+        ncot_v=v((roll, nodes, width), bf16),
+        ecot_v=v((roll, edges, width), bf16),
+        first_v=v(own, f32),
+        second_v=v(own, f32),
+        slots=v((slot_dev * depth, peers, rows, width), bf16),
+        halo=v((peers, roll * per_peer, width), bf16),
+        spread=v((peers, roll, per_peer, width), f32),
+        hput=v((peers, roll * per_peer, width), bf16),
+        hret=v((peers, roll * per_peer, width), bf16),
+        left_b=v((slot_dev, rows, width), bf16),
+        lput=v((slot_dev, peers, rows, rows), bf16),
+        lgot=v((slot_dev, peers, rows, rows), bf16),
+        right_b=v((slot_dev, width, width), bf16),
+        gather_t=v((padded, edges), bf16),
+        gather=v((edges, padded), bf16),
+        table=v((roll, padded, width), bf16),
+        eout_v=v((2, edges, width), bf16),
+        hidden_v=v((roll, edges, width), bf16),
+        slope_v=v((roll, edges, width), bf16),
+        normed_v=v((roll, edges, width), bf16),
+        inv_v=v((roll, edges, 1), f32),
+        summed_v=v((roll * nodes, width), bf16),
+        sc_own=v((roll * nodes, width), bf16),
+        sc_recv=v((roll * nodes, width), bf16),
+        nbase_v=v((roll * nodes, width), f32),
+        nout_v=v((roll, nodes, width), bf16),
+        ngrad_v=v((roll, nodes, width), bf16),
+        acc=v((8, 8, width), f32),
+        grad=v((NBLOCK, peers, rows, width), f32),
+        cast=v((NBLOCK, peers // 2, rows, width), bf16),
+        got_core=v((NBLOCK, peers // 2, rows, width), bf16),
+        put_one=v((NBLOCK, 2, rows, width), bf16),
+        got_one=v((NBLOCK, 2, rows, width), bf16),
+        put_two=v((NBLOCK, rows, width), bf16),
+        got_two=v((NBLOCK, rows, width), bf16),
+        put_up=v((depth, *own), bf16),
+        put_down=v((depth, *own), bf16),
+        got_up=v((depth, *own), bf16),
+        got_down=v((depth, *own), bf16),
+        full=v((slot_dev, peers, rows, width), bf16),
+        turned=v((slot_dev, peers, rows, width), bf16),
+        wnew_v=v(own, f32),
+        wcopy_v=v(own, bf16),
+        vstate_v=v((3, 8, width), f32),
+        norm_v=v(tile, f32),
+        vput=v((4, 8, width), f32),
+        vgot=v((3, 8, width), f32),
+        vz=v((depth, 8, width), f32),
+        sput=v(tile, f32),
+        sgot=v((peers, *tile), f32),
+        szput=v(tile, f32),
+        sz=v((depth, *tile), f32),
+        in_sem=dma((9,)),
+        out_sem=dma((6 + roll + 2 * slot_dev,)),
+        e_sem=dma((roll,)),
+        w_send=dma((7, depth)),
+        w_recv=dma((7, depth)),
+        wz_send=dma((2, depth)),
+        wz_recv=dma((depth,)),
+        h_send=dma((2, peers)),
+        h_recv=dma((2, peers)),
+        l_send=dma((peers,)),
+        l_recv=dma((peers,)),
+        r_send=dma((3 * NBLOCK,)),
+        r_recv=dma((3 * NBLOCK,)),
+        z_send=dma((2, depth, slot_dev)),
+        z_recv=dma((2, depth, slot_dev)),
+        g_send=dma((7, slot_dev)),
+        g_recv=dma((7, slot_dev)),
+        t_send=dma((7, slot_dev)),
+        t_recv=dma((7, slot_dev)),
+        v_send=dma((6,)),
+        v_recv=dma((6,)),
+        n_send=dma((peers + depth - 1,)),
+        n_recv=dma((peers + depth - 1,)),
+    )
+    names = (*ins, *outs, *scratch)
+    results = pl.pallas_call(
+        functools.partial(step_kernel, names),
+        out_shape=tuple(outs.values()),
+        in_specs=[spec for _, spec in ins.values()],
+        out_specs=(hbm,) * len(outs),
+        scratch_shapes=list(scratch.values()),
+        compiler_params=pltpu.CompilerParams(
+            vmem_limit_bytes=61 << 20, collective_id=0, has_side_effects=True
+        ),
+        name="step",
+    )(*(value for value, _ in ins.values()))
+    final = [*outs.values()][:-1]
+    return pl.pallas_call(
+        copy_kernel,
+        out_shape=(*final, shape((1,), f32)),
+        in_specs=[hbm] * len(final) + [vmem],
+        out_specs=(*([hbm] * len(final)), smem),
+        scratch_shapes=[v(out.shape, out.dtype) for out in final] + [dma((len(final),))] * 2,
+        compiler_params=pltpu.CompilerParams(vmem_limit_bytes=60 << 20),
+        name="results",
+    )(*results)
+
+
 def local(
     node_state,
     edge_state,
@@ -347,6 +1164,27 @@
     halo_rows = send_rows.shape[1]
     peers = lax.axis_size("node")
     per_peer = halo_rows // peers
+    if (lax.axis_size("dp"), peers) == (4, 8):
+        return whole_step(
+            node_state,
+            edge_state,
+            node_cotangent,
+            edge_cotangent,
+            send_rows,
+            edge_sender,
+            edge_receiver,
+            rollout_length,
+            slot_block,
+            step_count,
+            weight_slots,
+            moment_first,
+            moment_second,
+            basis_left,
+            basis_right,
+            vector_params,
+            vector_first,
+            vector_second,
+        )
     copies = lax.all_gather(weight_slots.astype(bf16), "node", axis=1, tiled=True)
     slots = lax.all_gather(copies, "dp", axis=0, tiled=True)
     back_onehot = (send_rows[0][:, None] == jnp.arange(nodes, dtype=jnp.int32)[None, :]).astype(bf16)

time: 425 us -> 127 us (0.30)
  waiting for transfers between devices: 269 us -> 0 us
  Pallas kernels: 39.9 us -> 125 us
  blocking collectives: 42 us -> 0 us
  matrix products: 23.1 us -> 0 us
  between operations: 18.6 us -> 1.46 us
  local copies, waits for them, and re-layouts: 11.6 us -> 0 us
  other arithmetic: 9.97 us -> 0 us
  starting transfers between devices: 8.24 us -> 0 us
    psum x1 -> x0, waiting for transfers between devices: 121 us -> none  [local(): summed, grad_vectors = lax.psum((grads, grad_vectors), ('dp', 'node'))]
    all_gather x2 -> x0, waiting for transfers between devices: 98.1 us -> none  [the longest x1 70.6 us: local(): slots = lax.all_gather(copies, 'dp', axis=0, tiled=True)]
    pallas_call x1 -> x2, Pallas kernels: 39.9 us -> 125 us  [the longest x1 118 us: whole_step(): pl.pallas_call(functools.partial(step_kernel, names), out_shape=tuple(out...]
    unnamed x5 -> x0, waiting for transfers between devices: 46.9 us -> none
    psum x1 -> x0, blocking collectives: 42 us -> none  [local(): summed, grad_vectors = lax.psum((grads, grad_vectors), ('dp', 'node'))]
    dot_general x7 -> x0, matrix products: 23.1 us -> none  [the longest x1 12.7 us: local(): owned_grads = jnp.einsum('bs,bij->sij', mine, summed, precision=highest)]
    all_to_all x2 -> x0, starting transfers between devices: 8.16 us -> none  [the longest x1 4.6 us: local(): lax.all_to_all(halo_back, 'node', split_axis=0, concat_axis=0, tiled=True)]
    reduce_sum x2 -> x0, other arithmetic: 6.18 us -> none  [the longest x1 5.57 us: local(): own_square = jnp.sum(summed * summed)]
  transfers between devices with their start and end apart: 6 -> 0, of which waited for: 5 -> 0; matrix products, arithmetic and copies ran while one was open for 9% -> 0% of each run, Pallas kernels for 0% -> 0%
where the time goes in v2:
time: 127 us
  Pallas kernels  125 us (98%)
  between operations  1.46 us (1%)
    pallas_call x1, Pallas kernels, whole_step(): pl.pallas_call(functools.partial(step_kernel, names), out_shape=tuple(out...  118 us
    pallas_call x1, Pallas kernels, whole_step(): pl.pallas_call(copy_kernel, out_shape=(*final, shape((1,), f32)), in_spec...  7.04 us

profile of v2, /device:TPU:1, one launch (start us, length us, event | category | flops | bytes accessed | tf_op | source)
XLA Modules:
  0.0 126.9 jit_solution(12651497918862048399)
XLA Ops:
  1.3 118.4 %step.1 = (bf16[1,4,128,512]{3,2,1,0:T(8,128)(2,1)}, bf16[1,4,768,512]{3,2,1,0:T(8,128)(2,1)}, bf16[1,4,128,512]{3,2,1,0:T(8,128)(2,1)}, bf16[1,4,768,512]{3,2,1...) custom-call(s32[1]{0:T(128)S(6)} %copy.28.refs_0_, ...), custom_call_target="tpu_custom_call" | custom-call | tf_op jit(solution)/shard_map/step/pallas_call | solution.py:1116
  119.7 7.0 %results.1 = (bf16[1,4,128,512]{3,2,1,0:T(8,128)(2,1)}, bf16[1,4,768,512]{3,2,1,0:T(8,128)(2,1)}, bf16[1,4,128,512]{3,2,1,0:T(8,128)(2,1)}, bf16[1,4,768,512]{3,...) custom-call(bf16[1,4,128,512]{3,2,1,0:T(8,128)(2,1)} %get-tuple-elem, ...), custom_call_target="tpu_custom_call" | custom-call | tf_op jit(solution)/shard_map/results/pallas_call | solution.py:1128

commit v3 on v2

--- a/solution.py
+++ b/solution.py
@@ -415,10 +415,9 @@
     halo = peers * per_peer
     known = nodes + halo
     padded = k.table.shape[1]
-    chunk = 384
+    chunk = edges
     pieces = edges // chunk
     going = []
-    leaving = []
 
     def launch(src, dst, send, recv, z, n):
         copy = remote(src, dst, send, recv, z, n)
@@ -427,11 +426,6 @@
 
     def landed(dst, recv):
         remote(dst, dst, recv, recv, p.z, p.sib).wait_recv()
-
-    def leave(src, dst, i):
-        copy = pltpu.make_async_copy(src, dst, k.out_sem.at[i])
-        copy.start()
-        leaving.append(copy)
 
     loads = []
     for i, (src, dst) in enumerate(
@@ -442,7 +436,7 @@
             (k.right_hbm, k.grad.at[:slot_dev]),
             (k.edge_hbm.at[0], k.edge_v),
             (k.ncot_hbm.at[0], k.ncot_v),
-            (k.ecot_hbm.at[0], k.ecot_v),
+            (k.ecot_hbm.at[0], k.egrad_v.at[0]),
             (k.first_hbm, k.first_v),
             (k.second_hbm, k.second_v),
         )
@@ -451,8 +445,8 @@
         loads[-1].start()
     greet_start(p, depth, peers)
 
-    def buf(z, n):
-        return k.slots.at[pl.ds(slot_dev * z, slot_dev), n]
+    def buf(slot, n):
+        return k.slots.at[slot, n]
 
     wsems = (k.w_send, k.w_recv)
     order = []
@@ -460,19 +454,20 @@
     def arrive(j):
         z_of = 0
         for z in range(depth):
-            z_of = z_of + jnp.where(p.z == z, ORDER[z][j], 0)
-        order.append(z_of)
-        piece = buf(z_of, p.n)
-        if j:
-            remote(piece, piece, k.wz_send.at[0, z_of], k.wz_recv.at[z_of], p.z, p.n).wait_recv()
+            z_of = z_of + jnp.where(p.z == z, ORDER[z][j // slot_dev], 0)
+        slot = z_of * slot_dev + j % slot_dev
+        order.append(slot)
+        piece = buf(slot, p.n)
+        if j >= slot_dev:
+            remote(piece, piece, k.wz_send.at[0, slot], k.wz_recv.at[slot], p.z, p.n).wait_recv()
         for i, test, to in (
             (0, (z_of <= p.z) & (p.z < depth - 1), p.z + 1),
             (1, (z_of >= p.z) & (p.z > 0), p.z - 1),
         ):
-            copy = remote(piece, piece, k.wz_send.at[i, z_of], k.wz_recv.at[z_of], to, p.n)
+            copy = remote(piece, piece, k.wz_send.at[i, slot], k.wz_recv.at[slot], to, p.n)
             pl.when(test)(copy.start)
             going.append((copy, test))
-        going.extend((copy, None) for copy in gather_start(p, buf, z_of, wsems))
+        going.extend((copy, None) for copy in gather_start(p, buf, slot, wsems))
 
     def side(j):
         going.extend((copy, None) for copy in gather_side(p, buf, order[j], wsems))
@@ -483,58 +478,53 @@
     loads[0].wait()
     k.slots[pl.ds(slot_dev * p.z, slot_dev), p.n] = k.weight_v[...].astype(bf16)
     greet_end(depth, peers)
-    arrive(0)
+
+    def rounds(*names):
+        for name in names:
+            {"a": arrive, "s": side, "f": far}[name[0]](int(name[1:]))
+
+    rounds("a0", "a1")
     loads[1].wait()
     node_ids = lax.broadcasted_iota(jnp.int32, (nodes, halo), 0)
     pick_t = jnp.where(node_ids == k.rows_ref[...], 1.0, 0.0).astype(bf16)
     for t in range(roll):
-        k.spread[:, t] = dot(pick_t.T, k.node_v[t]).reshape(peers, per_peer, width)
+        k.spread[:, t] = dot_ta(pick_t, k.node_v[t]).reshape(peers, per_peer, width)
     k.hput[...] = k.spread[...].reshape(peers, roll * per_peer, width).astype(bf16)
     k.halo[p.n] = k.hput[p.n]
+    rounds("a2", "a3", "s0", "s1")
     hsent = []
     for i in range(1, peers):
         to = lax.rem(p.n + i, peers)
         hsent.append(remote(k.hput.at[to], k.halo.at[p.n], k.h_send.at[0, i], k.h_recv.at[0, i], p.z, to))
         hsent[-1].start()
-    arrive(1)
-    side(0)
     loads[2].wait()
     for s in range(slot_dev):
-        k.left_b[s] = k.grad[2, s].astype(bf16)
+        k.pre[2 * slot_dev + s, p.n] = k.grad[2, s].astype(bf16)
         for m in range(peers):
             k.lput[s, m] = k.grad[2, s, :, m * rows : (m + 1) * rows].astype(bf16)
     k.lgot[:, p.n] = k.lput[:, p.n]
-    for i in range(1, peers):
-        to = lax.rem(p.n + i, peers)
-        launch(k.lput.at[:, to], k.lgot.at[:, p.n], k.l_send.at[i], k.l_recv.at[i], p.z, to)
-    arrive(2)
-    side(1)
-    far(0)
+    rounds("a4", "a5", "s2", "s3", "f0", "f1")
     ids = lax.broadcasted_iota(jnp.int32, (padded, edges), 0)
     onehot = (ids == k.sender_ref[...].reshape(1, edges)) | (
         ids == k.receiver_ref[...].reshape(1, edges) + known
     )
     onehot = jnp.where(onehot, 1.0, 0.0).astype(f32)
     k.gather_t[...] = onehot.astype(bf16)
-    arrive(3)
-    side(2)
-    far(1)
+    rounds("a6", "a7", "s4", "s5", "f2", "f3")
     k.gather[...] = onehot.T.astype(bf16)
     k.table[:, known + nodes :] = jnp.zeros((roll, padded - known - nodes, width), bf16)
     k.acc[...] = jnp.zeros_like(k.acc)
-    side(3)
-    far(2)
+    rounds("s6", "s7", "f4", "f5")
     loads[3].wait()
     for s in range(slot_dev):
         k.right_b[s] = k.grad[s].reshape(width, width).astype(bf16)
-    far(3)
+    rounds("f6", "f7")
     for copy in hsent:
         copy.wait_send()
     for i in range(1, peers):
         landed(k.halo.at[0], k.h_recv.at[0, i])
-        landed(k.lgot.at[:, 0], k.l_recv.at[i])
-    for j in range(depth):
-        gather_end(p, buf, order[j], wsems)
+    for slot in order:
+        gather_end(p, buf, slot, wsems)
 
     slot_of = []
     for b in range(NBLOCK):
@@ -565,17 +555,22 @@
         k.table[t, known : known + nodes] = own_recv[t * nodes : (t + 1) * nodes].astype(bf16)
     loads[4].wait()
 
-    def edge_out(t):
-        return pltpu.make_async_copy(k.eout_v.at[t % 2], k.eout_hbm.at[0, t], k.e_sem.at[t])
+    for i in range(1, peers):
+        to = lax.rem(p.n + i, peers)
+        launch(k.lput.at[:, to], k.lgot.at[:, p.n], k.l_send.at[i], k.l_recv.at[i], p.z, to)
+    loads[7].wait()
+    loads[8].wait()
+    psems = (k.p_send, k.p_recv)
+    early = range(3 * slot_dev)
+    pbuf = lambda i, n: k.pre.at[i, n]
+    for s in range(slot_dev):
+        k.pre[s, p.n] = k.first_v[s].astype(bf16)
+        k.pre[slot_dev + s, p.n] = k.second_v[s].astype(bf16)
+    for i in early:
+        going.extend((copy, None) for copy in gather_start(p, pbuf, i, psems))
 
     def forward(t, carry):
         lv = live(t)
-        slot = t % 2
-
-        @pl.when(t >= 2)
-        def _():
-            edge_out(t - 2).wait()
-
         total = jnp.zeros((nodes, width), f32)
         for c in range(pieces):
             at = pl.ds(c * chunk, chunk)
@@ -587,10 +582,9 @@
             k.normed_v[t, at] = normed.astype(bf16)
             k.inv_v[t, at] = inverse
             new = edge.astype(f32) + (normed * vec[2:3] + vec[3:4])
-            k.eout_v[slot, at] = (new * lv).astype(bf16)
+            k.eout_v[0, t, at] = (new * lv).astype(bf16)
             total += dot(k.gather_t[known : known + nodes, at], new.astype(bf16))
         k.summed_v[pl.ds(t * nodes, nodes)] = total.astype(bf16)
-        edge_out(t).start()
         return carry
 
     lax.fori_loop(0, roll, forward, 0)
@@ -648,8 +642,7 @@
     row_t = lax.broadcasted_iota(jnp.int32, (roll * nodes, 1), 0) // nodes
     row_live = jnp.where(row_t < rollout, 1.0, 0.0).astype(f32)
     new = flat_nodes().astype(f32) + (normed * vec[6:7] + vec[7:8])
-    k.nout_v[...] = (new * row_live).astype(bf16).reshape(roll, nodes, width)
-    leave(k.nout_v, k.nout_hbm.at[0], 0)
+    k.nout_v[0] = (new * row_live).astype(bf16).reshape(roll, nodes, width)
     loads[5].wait()
     d_new = k.ncot_v[...].reshape(roll * nodes, width).astype(f32) * row_live
     k.acc[6] = eights(d_new * normed)
@@ -665,7 +658,9 @@
     put_grad(5, dot_ta(summed, d_before))
     to_core(5)
     k.summed_v[...] = dot_tb(d_before, weight(5)).astype(bf16)
-    k.nbase_v[...] = d_new + dot_tb(d_before, weight(4))
+    k.table[:, 2 * nodes : 3 * nodes] = d_before.reshape(roll, nodes, width)
+    for i in early:
+        going.extend((copy, None) for copy in gather_side(p, pbuf, i, psems))
     k.grad[0] = jnp.zeros((peers, rows, width), f32)
     k.grad[3] = jnp.zeros((peers, rows, width), f32)
     loads[6].wait()
@@ -674,10 +669,10 @@
         lv = live(t)
         for c in range(pieces):
             at = pl.ds(c * chunk, chunk)
-            d_new = k.ecot_v[t, at].astype(f32) * lv + dot(
+            d_new = k.egrad_v[0, t, at].astype(f32) * lv + dot(
                 k.gather[at, known : known + nodes], k.summed_v[pl.ds(t * nodes, nodes)]
             )
-            k.ecot_v[t, at] = d_new.astype(bf16)
+            k.egrad_v[0, t, at] = d_new.astype(bf16)
             normed = k.normed_v[t, at].astype(f32)
             k.acc[2] += eights(d_new * normed)
             k.acc[3] += eights(d_new)
@@ -690,8 +685,8 @@
         k.grad[3] += dot_ta(k.hidden_v[t], k.normed_v[t]).reshape(peers, rows, width)
         k.grad[0] += dot_ta(k.edge_v[t], k.slope_v[t]).reshape(peers, rows, width)
         scattered = dot(k.gather_t[...], k.slope_v[t])
-        k.sc_own[pl.ds(t * nodes, nodes)] = scattered[:nodes].astype(bf16)
-        k.sc_recv[pl.ds(t * nodes, nodes)] = scattered[known : known + nodes].astype(bf16)
+        k.table[t, :nodes] = scattered[:nodes].astype(bf16)
+        k.table[t, nodes : 2 * nodes] = scattered[known : known + nodes].astype(bf16)
         k.spread[:, t] = scattered[nodes:known].reshape(peers, per_peer, width)
         for step, work in enumerate((to_first, to_second, settle)):
 
@@ -710,43 +705,44 @@
     to_core(3)
     to_core(0)
     k.hput[...] = k.spread[...].reshape(peers, roll * per_peer, width).astype(bf16)
-    put_grad(1, dot_ta(flat_nodes(), k.sc_own[...]) + dot_ta(halo_flat, k.hput[...].reshape(roll * halo, width)))
+    def kept(i):
+        return k.table[:, i * nodes : (i + 1) * nodes].reshape(roll * nodes, width)
+
+    put_grad(1, dot_ta(flat_nodes(), kept(0)) + dot_ta(halo_flat, k.hput[...].reshape(roll * halo, width)))
     to_core(1)
-    put_grad(2, dot_ta(flat_nodes(), k.sc_recv[...]))
+    to_first(3)
+    put_grad(2, dot_ta(flat_nodes(), kept(1)))
     to_core(2)
+    to_first(0)
     k.vput[0] = jnp.sum(k.acc[...], axis=1)
     launch(k.vput.at[0], k.vgot.at[0], k.v_send.at[0], k.v_recv.at[0], p.z, p.sib)
+    to_first(1)
+    to_second(3)
+    to_first(2)
+    landed(k.vgot.at[0], k.v_recv.at[0])
+    k.vput[1] = k.vput[0] + k.vgot[0]
+    launch(k.vput.at[1], k.vgot.at[1], k.v_send.at[1], k.v_recv.at[1], p.z, p.xn)
+    to_second(0)
+    for i in early:
+        going.extend((copy, None) for copy in gather_far(p, pbuf, i, psems))
+
+    def edge_gradient(t):
+        for c in range(pieces):
+            at = pl.ds(c * chunk, chunk)
+            grown = k.egrad_v[0, t, at].astype(f32) + dot_tb(k.slope_v[t, at], weight(0))
+            k.egrad_v[0, t, at] = grown.astype(bf16)
+
+    to_second(1)
+    settle(3)
+    to_second(2)
+    settle(0)
+    landed(k.vgot.at[1], k.v_recv.at[1])
+    k.vput[2] = k.vput[1] + k.vgot[1]
+    launch(k.vput.at[2], k.vgot.at[2], k.v_send.at[2], k.v_recv.at[2], p.z, p.yn)
     for i in range(1, peers):
         to = lax.rem(p.n + i, peers)
         launch(k.hput.at[to], k.hret.at[p.n], k.h_send.at[1, i], k.h_recv.at[1, i], p.z, to)
     k.hret[p.n] = k.hput[p.n]
-    to_first(3)
-    to_first(0)
-
-    def edge_gradient(t):
-        for c in range(pieces):
-            at = pl.ds(c * chunk, chunk)
-            grown = k.ecot_v[t, at].astype(f32) + dot_tb(k.slope_v[t, at], weight(0))
-            k.ecot_v[t, at] = grown.astype(bf16)
-        leave(k.ecot_v.at[t], k.egrad_hbm.at[0, t], 2 + t)
-
-    edge_gradient(0)
-    to_first(1)
-    to_first(2)
-    to_second(3)
-    to_second(0)
-    landed(k.vgot.at[0], k.v_recv.at[0])
-    k.vput[1] = k.vput[0] + k.vgot[0]
-    launch(k.vput.at[1], k.vgot.at[1], k.v_send.at[1], k.v_recv.at[1], p.z, p.xn)
-    edge_gradient(1)
-    to_second(1)
-    to_second(2)
-    settle(3)
-    settle(0)
-    landed(k.vgot.at[1], k.v_recv.at[1])
-    k.vput[2] = k.vput[1] + k.vgot[1]
-    launch(k.vput.at[2], k.vgot.at[2], k.v_send.at[2], k.v_recv.at[2], p.z, p.yn)
-    edge_gradient(2)
     settle(1)
     settle(2)
 
@@ -786,14 +782,32 @@
                         p.n,
                     ).start()
 
-    @pl.when(p.z < depth // 2)
+    @pl.when(p.z == 0)
     def _():
         pass_on(0)
-        pass_on(1)
-
-    @pl.when(p.z >= depth // 2)
+
+    @pl.when(p.z == depth - 1)
     def _():
         pass_on(1)
+
+    edge_gradient(0)
+
+    @pl.when(p.z == 1)
+    def _():
+        pass_on(0)
+
+    @pl.when(p.z == depth - 2)
+    def _():
+        pass_on(1)
+
+    edge_gradient(1)
+
+    @pl.when(p.z == 1)
+    def _():
+        pass_on(1)
+
+    @pl.when(p.z == depth - 2)
+    def _():
         pass_on(0)
 
     landed(k.vgot.at[2], k.v_recv.at[2])
@@ -802,18 +816,7 @@
     for i in range(1, depth):
         to = lax.rem(p.z + i, depth)
         launch(k.vput.at[3], k.vz.at[p.z], k.v_send.at[2 + i], k.v_recv.at[2 + i], to, p.n)
-    edge_gradient(3)
-    for i in range(1, peers):
-        landed(k.hret.at[0], k.h_recv.at[1, i])
-    back = k.hret[...].astype(f32).reshape(peers, roll, per_peer, width)
-    for t in range(roll):
-        at = pl.ds(t * nodes, nodes)
-        rows_t = back[:, t].reshape(halo, width).astype(bf16)
-        k.sc_own[at] = (k.sc_own[at].astype(f32) + dot(pick_t, rows_t)).astype(bf16)
-    grown = k.nbase_v[...] + dot_tb(k.sc_own[...], weight(1)) + dot_tb(k.sc_recv[...], weight(2))
-    k.ngrad_v[...] = grown.astype(bf16).reshape(roll, nodes, width)
-    leave(k.ngrad_v, k.ngrad_hbm.at[0], 1)
-
+    edge_gradient(2)
     square = jnp.zeros((8, width), f32)
     gsems = (k.g_send, k.g_recv)
     gbuf = lambda s, n: k.full.at[s, n]
@@ -839,6 +842,7 @@
     for i in range(1, peers):
         to = lax.rem(p.n + i, peers)
         launch(k.sput, k.sgot.at[p.n], k.n_send.at[i], k.n_recv.at[i], p.z, to)
+    edge_gradient(3)
 
     def collect(buffer, sems, finish):
         for s in range(slot_dev):
@@ -857,46 +861,71 @@
         to = lax.rem(p.z + i, depth)
         launch(k.szput, k.sz.at[p.z], k.n_send.at[peers - 1 + i], k.n_recv.at[peers - 1 + i], to, p.n)
 
-    rotated = [None] * slot_dev
-
-    def rotate(s):
-        part_left = dot(k.left_b[s], k.full[s].reshape(width, width))
-        rotated[s] = dot(part_left.astype(bf16), k.right_b[s])
-
-    collect(gbuf, gsems, rotate)
-    for i in range(1, depth):
-        landed(k.vz.at[0], k.v_recv.at[2 + i])
-        landed(k.sz.at[0], k.n_recv.at[peers - 1 + i])
-    grad_vectors = k.vz[0] + k.vz[1] + k.vz[2] + k.vz[3]
-    square_sum = jnp.sum(k.sz[0] + k.sz[1] + k.sz[2] + k.sz[3], keepdims=True).reshape(1, 1)
-    square_sum = square_sum + jnp.sum(grad_vectors * grad_vectors, keepdims=True).reshape(1, 1)
-    grad_norm = jnp.sqrt(square_sum)
-    k.norm_v[...] = jnp.broadcast_to(grad_norm, k.norm_v.shape)
-    leave(k.norm_v, k.norm_hbm, 2 + roll)
     limit = math.sqrt(NBLOCK * width * width + 8 * width)
-    clip = jnp.minimum(1.0, limit / grad_norm)
+    found = []
+
+    for i in range(1, peers):
+        landed(k.hret.at[0], k.h_recv.at[1, i])
+    back = k.hret[...].astype(f32).reshape(peers, roll, per_peer, width)
+    for t in range(roll):
+        rows_t = back[:, t].reshape(halo, width).astype(bf16)
+        k.table[t, :nodes] = (k.table[t, :nodes].astype(f32) + dot(pick_t, rows_t)).astype(bf16)
+    grown = k.ncot_v[...].reshape(roll * nodes, width).astype(f32) * row_live
+    grown = grown + dot_tb(kept(0), weight(1)) + dot_tb(kept(1), weight(2)) + dot_tb(kept(2), weight(4))
+    k.ngrad_v[0] = grown.astype(bf16).reshape(roll, nodes, width)
 
     def fix(beta, step):
         return 1.0 - jnp.exp2(math.log2(beta) * jnp.full((1, 1), step, jnp.int32).astype(f32))
 
-    tsems = (k.t_send, k.t_recv)
-    tbuf = lambda s, n: k.turned.at[s, n]
-    loads[7].wait()
-    loads[8].wait()
-    for s in range(slot_dev):
+    def norm():
+        for i in range(1, depth):
+            landed(k.vz.at[0], k.v_recv.at[2 + i])
+            landed(k.sz.at[0], k.n_recv.at[peers - 1 + i])
+        vectors = k.vz[0] + k.vz[1] + k.vz[2] + k.vz[3]
+        square_sum = jnp.sum(k.sz[0] + k.sz[1] + k.sz[2] + k.sz[3], keepdims=True).reshape(1, 1)
+        square_sum = square_sum + jnp.sum(vectors * vectors, keepdims=True).reshape(1, 1)
+        value = jnp.sqrt(square_sum)
+        k.norm_v[...] = jnp.broadcast_to(value, k.norm_v.shape)
+        found.extend((vectors, jnp.minimum(1.0, limit / value)))
+
+    def advance(s):
+        part_left = dot(k.pre[2 * slot_dev + s].reshape(width, width), k.full[s].reshape(width, width))
+        rotated = dot(part_left.astype(bf16), k.right_b[s])
+        if s == 0:
+            norm()
+        k.grad[s] = rotated.reshape(peers, rows, width)
         step = k.step_ref[p.z * slot_dev + s]
-        spun = rotated[s] * clip
-        one = beta_first * k.first_v[s] + (1.0 - beta_first) * spun
-        two = beta_second * k.second_v[s] + (1.0 - beta_second) * spun * spun
+        fix_one, fix_two = fix(beta_first, step), fix(beta_second, step)
+        clip = found[1]
+
+        def moments(first, second, turn):
+            spun = turn * clip
+            return (
+                beta_first * first + (1.0 - beta_first) * spun,
+                beta_second * second + (1.0 - beta_second) * spun * spun,
+            )
+
+        one, two = moments(
+            k.pre[s].reshape(width, width).astype(f32),
+            k.pre[slot_dev + s].reshape(width, width).astype(f32),
+            rotated,
+        )
+        direction = adam_direction(one, two, fix_one, fix_two).astype(bf16)
+        turned = dot_tb(direction, k.right_b[s]).astype(bf16)
+        reverted = dot_ta(k.lgot[s].reshape(width, rows), turned)
+        new = k.weight_v[s] - rate_matrix * (reverted + weight_decay * k.weight_v[s])
+        k.wnew_v[s] = new
+        k.wcopy_v[s] = new.astype(bf16)
+        one, two = moments(k.first_v[s], k.second_v[s], k.grad[s, p.n])
         k.first_v[s] = one
         k.second_v[s] = two
-        direction = adam_direction(one, two, fix(beta_first, step), fix(beta_second, step))
-        k.turned[s, p.n] = dot_tb(direction.astype(bf16), k.right_b[s]).astype(bf16)
-        for copy in gather_start(p, tbuf, s, tsems):
-            going.append((copy, None))
-    leave(k.first_v, k.first_out, 3 + roll)
-    leave(k.second_v, k.second_out, 4 + roll)
-
+
+    for i in range(1, peers):
+        landed(k.lgot.at[:, 0], k.l_recv.at[i])
+    for i in early:
+        gather_end(p, pbuf, i, psems)
+    collect(gbuf, gsems, advance)
+    grad_vectors, clip = found
     step = k.step_ref[depth * slot_dev]
     spun = grad_vectors * clip
     one = beta_first * k.vfirst_ref[...] + (1.0 - beta_first) * spun
@@ -906,18 +935,6 @@
     )
     k.vstate_v[1] = one
     k.vstate_v[2] = two
-    leave(k.vstate_v, k.vstate_hbm, 5 + roll)
-
-    def finish(s):
-        left_back = k.lgot[s].reshape(width, rows)
-        reverted = dot_ta(left_back, k.turned[s].reshape(width, width))
-        new = k.weight_v[s] - rate_matrix * (reverted + weight_decay * k.weight_v[s])
-        k.wnew_v[s] = new
-        k.wcopy_v[s] = new.astype(bf16)
-        leave(k.wnew_v.at[s], k.wnew_hbm.at[s], 6 + roll + s)
-        leave(k.wcopy_v.at[s], k.wcopy_hbm.at[s], 6 + roll + slot_dev + s)
-
-    collect(tbuf, tsems, finish)
 
     for copy, test in going:
         if test is None:
@@ -942,26 +959,17 @@
                     p.sib,
                 )
                 pl.when(test)(sent.wait_send)
-    for t in (roll - 2, roll - 1):
-        edge_out(t).wait()
-    for copy in leaving:
-        copy.wait()
-
-
-def copy_kernel(*refs):
-    count = 9
-    sources, norm, targets, norm_out = refs[:count], refs[count], refs[count + 1 : -count - 3], refs[-count - 3]
-    stage, in_sem, out_sem = refs[-count - 2 : -2], refs[-2], refs[-1]
-    first, second = [], []
+
+
+def store_kernel(*refs):
+    count = (len(refs) - 3) // 2
+    norm, norm_out, sem = refs[count], refs[-2], refs[-1]
+    copies = []
     for i in range(count):
-        first.append(pltpu.make_async_copy(sources[i], stage[i], in_sem.at[i]))
-        second.append(pltpu.make_async_copy(stage[i], targets[i], out_sem.at[i]))
-        first[-1].start()
+        copies.append(pltpu.make_async_copy(refs[i], refs[count + 1 + i], sem.at[i]))
+        copies[-1].start()
     norm_out[0] = norm[0, 0]
-    for i in range(count):
-        first[i].wait()
-        second[i].start()
-    for copy in second:
+    for copy in copies:
         copy.wait()
 
 
@@ -1020,16 +1028,16 @@
         vsecond_ref=(vector_second, vmem),
     )
     outs = dict(
-        nout_hbm=shape(node_state.shape, bf16),
-        eout_hbm=shape(edge_state.shape, bf16),
-        ngrad_hbm=shape(node_state.shape, bf16),
-        egrad_hbm=shape(edge_state.shape, bf16),
-        first_out=shape(own, f32),
-        second_out=shape(own, f32),
-        wnew_hbm=shape(own, f32),
-        wcopy_hbm=shape(own, bf16),
-        vstate_hbm=shape((3, 8, width), f32),
-        norm_hbm=shape(tile, f32),
+        nout_v=shape(node_state.shape, bf16),
+        eout_v=shape(edge_state.shape, bf16),
+        ngrad_v=shape(node_state.shape, bf16),
+        egrad_v=shape(edge_state.shape, bf16),
+        first_v=shape(own, f32),
+        second_v=shape(own, f32),
+        wnew_v=shape(own, f32),
+        wcopy_v=shape(own, bf16),
+        vstate_v=shape((3, 8, width), f32),
+        norm_v=shape(tile, f32),
     )
     v = pltpu.VMEM
     scratch = dict(
@@ -1037,32 +1045,23 @@
         node_v=v((roll, nodes, width), bf16),
         edge_v=v((roll, edges, width), bf16),
         ncot_v=v((roll, nodes, width), bf16),
-        ecot_v=v((roll, edges, width), bf16),
-        first_v=v(own, f32),
-        second_v=v(own, f32),
         slots=v((slot_dev * depth, peers, rows, width), bf16),
         halo=v((peers, roll * per_peer, width), bf16),
         spread=v((peers, roll, per_peer, width), f32),
         hput=v((peers, roll * per_peer, width), bf16),
         hret=v((peers, roll * per_peer, width), bf16),
-        left_b=v((slot_dev, rows, width), bf16),
+        pre=v((3 * slot_dev, peers, rows, width), bf16),
         lput=v((slot_dev, peers, rows, rows), bf16),
         lgot=v((slot_dev, peers, rows, rows), bf16),
         right_b=v((slot_dev, width, width), bf16),
         gather_t=v((padded, edges), bf16),
         gather=v((edges, padded), bf16),
         table=v((roll, padded, width), bf16),
-        eout_v=v((2, edges, width), bf16),
         hidden_v=v((roll, edges, width), bf16),
         slope_v=v((roll, edges, width), bf16),
         normed_v=v((roll, edges, width), bf16),
         inv_v=v((roll, edges, 1), f32),
         summed_v=v((roll * nodes, width), bf16),
-        sc_own=v((roll * nodes, width), bf16),
-        sc_recv=v((roll * nodes, width), bf16),
-        nbase_v=v((roll * nodes, width), f32),
-        nout_v=v((roll, nodes, width), bf16),
-        ngrad_v=v((roll, nodes, width), bf16),
         acc=v((8, 8, width), f32),
         grad=v((NBLOCK, peers, rows, width), f32),
         cast=v((NBLOCK, peers // 2, rows, width), bf16),
@@ -1076,11 +1075,6 @@
         got_up=v((depth, *own), bf16),
         got_down=v((depth, *own), bf16),
         full=v((slot_dev, peers, rows, width), bf16),
-        turned=v((slot_dev, peers, rows, width), bf16),
-        wnew_v=v(own, f32),
-        wcopy_v=v(own, bf16),
-        vstate_v=v((3, 8, width), f32),
-        norm_v=v(tile, f32),
         vput=v((4, 8, width), f32),
         vgot=v((3, 8, width), f32),
         vz=v((depth, 8, width), f32),
@@ -1089,12 +1083,10 @@
         szput=v(tile, f32),
         sz=v((depth, *tile), f32),
         in_sem=dma((9,)),
-        out_sem=dma((6 + roll + 2 * slot_dev,)),
-        e_sem=dma((roll,)),
-        w_send=dma((7, depth)),
-        w_recv=dma((7, depth)),
-        wz_send=dma((2, depth)),
-        wz_recv=dma((depth,)),
+        w_send=dma((7, depth * slot_dev)),
+        w_recv=dma((7, depth * slot_dev)),
+        wz_send=dma((2, depth * slot_dev)),
+        wz_recv=dma((depth * slot_dev,)),
         h_send=dma((2, peers)),
         h_recv=dma((2, peers)),
         l_send=dma((peers,)),
@@ -1105,8 +1097,8 @@
         z_recv=dma((2, depth, slot_dev)),
         g_send=dma((7, slot_dev)),
         g_recv=dma((7, slot_dev)),
-        t_send=dma((7, slot_dev)),
-        t_recv=dma((7, slot_dev)),
+        p_send=dma((7, 3 * slot_dev)),
+        p_recv=dma((7, 3 * slot_dev)),
         v_send=dma((6,)),
         v_recv=dma((6,)),
         n_send=dma((peers + depth - 1,)),
@@ -1115,23 +1107,28 @@
     names = (*ins, *outs, *scratch)
     results = pl.pallas_call(
         functools.partial(step_kernel, names),
-        out_shape=tuple(outs.values()),
+        out_shape=tuple(pltpu.VMEM(out.shape, out.dtype) for out in outs.values()),
         in_specs=[spec for _, spec in ins.values()],
-        out_specs=(hbm,) * len(outs),
+        out_specs=(vmem,) * len(outs),
         scratch_shapes=list(scratch.values()),
         compiler_params=pltpu.CompilerParams(
-            vmem_limit_bytes=61 << 20, collective_id=0, has_side_effects=True
+            vmem_limit_bytes=52 << 20, collective_id=0, has_side_effects=True
         ),
         name="step",
-    )(*(value for value, _ in ins.values()))
+    )(
+        *(
+            pltpu.with_memory_space_constraint(value, pltpu.HBM) if spec is hbm else value
+            for value, spec in ins.values()
+        )
+    )
     final = [*outs.values()][:-1]
     return pl.pallas_call(
-        copy_kernel,
+        store_kernel,
         out_shape=(*final, shape((1,), f32)),
-        in_specs=[hbm] * len(final) + [vmem],
+        in_specs=[vmem] * len(outs),
         out_specs=(*([hbm] * len(final)), smem),
-        scratch_shapes=[v(out.shape, out.dtype) for out in final] + [dma((len(final),))] * 2,
-        compiler_params=pltpu.CompilerParams(vmem_limit_bytes=60 << 20),
+        scratch_shapes=[dma((len(final),))],
+        compiler_params=pltpu.CompilerParams(vmem_limit_bytes=40 << 20),
         name="results",
     )(*results)
 

time: 127 us -> 116 us (0.913)
  Pallas kernels: 125 us -> 114 us
    pallas_call x2, Pallas kernels: 125 us -> 114 us  [the longest x1 110 us: whole_step(): pl.pallas_call(functools.partial(step_kernel, names), out_shape=tuple((pl...]
where the time goes in v3:
time: 116 us
  Pallas kernels  114 us (98%)
  between operations  1.46 us (1%)
    pallas_call x1, Pallas kernels, whole_step(): pl.pallas_call(functools.partial(step_kernel, names), out_shape=tuple((pl...  110 us
    pallas_call x1, Pallas kernels, whole_step(): pl.pallas_call(store_kernel, out_shape=(*final, shape((1,), f32)), in_spe...  3.83 us

profile of v3, /device:TPU:1, one launch (start us, length us, event | category | flops | bytes accessed | tf_op | source)
XLA Modules:
  0.0 115.7 jit_solution(14472066771380533178)
XLA Ops:
  1.3 110.4 %step.1 = (bf16[1,4,128,512]{3,2,1,0:T(8,128)(2,1)S(1)}, bf16[1,4,768,512]{3,2,1,0:T(8,128)(2,1)S(1)}, bf16[1,4,128,512]{3,2,1,0:T(8,128)(2,1)S(1)}, bf16[1,4,76...) custom-call(s32[1]{0:T(128)S(6)} %copy.28.refs_0_, ...), custom_call_target="tpu_custom_call" | custom-call | tf_op jit(solution)/shard_map/step/pallas_call | solution.py:1108
  111.7 3.8 %results.1 = (bf16[1,4,128,512]{3,2,1,0:T(8,128)(2,1)}, bf16[1,4,768,512]{3,2,1,0:T(8,128)(2,1)}, bf16[1,4,128,512]{3,2,1,0:T(8,128)(2,1)}, bf16[1,4,768,512]{3,...) custom-call(bf16[1,4,128,512]{3,2,1,0:T(8,128)(2,1)S(1)} %get-tuple-, ...), custom_call_target="tpu_custom_call" | custom-call | tf_op jit(solution)/shard_map/results/pallas_call | solution.py:1125

commit v4 on v3

--- a/solution.py
+++ b/solution.py
@@ -445,44 +445,98 @@
         loads[-1].start()
     greet_start(p, depth, peers)
 
-    def buf(slot, n):
-        return k.slots.at[slot, n]
+    cut = rows * 3 // 4
+
+    def shard(j):
+        top = cut if j % slot_dev == slot_dev - 1 else rows
+        return lambda slot, n: k.slots.at[slot, n // 2, lax.rem(n, 2), :top]
+
+    def rest(slot):
+        return k.slots.at[slot, :, p.c, cut:]
+
+    planes = []
+    for j in range(depth):
+        z_of = 0
+        for z in range(depth):
+            z_of = z_of + jnp.where(p.z == z, ORDER[z][j], 0)
+        planes.append(z_of)
+
+    def along_z(z_of):
+        return (
+            (0, (z_of <= p.z) & (p.z < depth - 1) & (p.z - z_of < depth - 2), p.z + 1),
+            (1, (z_of >= p.z) & (p.z > 0) & (z_of - p.z < depth - 2), p.z - 1),
+            (2, (z_of == p.z) & ((p.z == 0) | (p.z == depth - 1)), depth - 1 - p.z),
+        )
+
+    def rest_hop(s, i):
+        own = k.slots.at[p.z * slot_dev + s, p.n // 2, p.c, cut:]
+        to = (p.xn, p.yn, p.diag)[i]
+        return remote(own, own, k.b_send.at[i, s], k.b_recv.at[i, s], p.z, to)
+
+    def rest_start(s):
+        for i in range(3):
+            rest_hop(s, i).start()
+            going.append((rest_hop(s, i), None))
+
+    def rest_pass(j, s):
+        slot = planes[j] * slot_dev + s
+        ref = rest(slot)
+        if j == 0:
+            for i in range(3):
+                rest_hop(s, i).wait_recv()
+        else:
+            remote(ref, ref, k.bz_send.at[0, slot], k.bz_recv.at[slot], p.z, p.sib).wait_recv()
+        for i, test, to in along_z(planes[j]):
+            if i == 2 and j:
+                continue
+            copy = remote(ref, ref, k.bz_send.at[i, slot], k.bz_recv.at[slot], to, p.n)
+            pl.when(test)(copy.start)
+            going.append((copy, test))
+        copy = remote(ref, ref, k.bs_send.at[slot], k.bs_recv.at[slot], p.z, p.sib)
+        copy.start()
+        going.append((copy, None))
+
+    def rest_end(slot):
+        ref = rest(slot)
+        remote(ref, ref, k.bs_send.at[slot], k.bs_recv.at[slot], p.z, p.sib).wait_recv()
 
     wsems = (k.w_send, k.w_recv)
     order = []
 
     def arrive(j):
-        z_of = 0
-        for z in range(depth):
-            z_of = z_of + jnp.where(p.z == z, ORDER[z][j // slot_dev], 0)
+        z_of = planes[j // slot_dev]
         slot = z_of * slot_dev + j % slot_dev
         order.append(slot)
-        piece = buf(slot, p.n)
+        piece = shard(j)(slot, p.n)
         if j >= slot_dev:
             remote(piece, piece, k.wz_send.at[0, slot], k.wz_recv.at[slot], p.z, p.n).wait_recv()
-        for i, test, to in (
-            (0, (z_of <= p.z) & (p.z < depth - 1), p.z + 1),
-            (1, (z_of >= p.z) & (p.z > 0), p.z - 1),
-        ):
+        for i, test, to in along_z(z_of):
+            if i == 2 and j >= slot_dev:
+                continue
             copy = remote(piece, piece, k.wz_send.at[i, slot], k.wz_recv.at[slot], to, p.n)
             pl.when(test)(copy.start)
             going.append((copy, test))
-        going.extend((copy, None) for copy in gather_start(p, buf, slot, wsems))
+        going.extend((copy, None) for copy in gather_start(p, shard(j), slot, wsems))
 
     def side(j):
-        going.extend((copy, None) for copy in gather_side(p, buf, order[j], wsems))
+        going.extend((copy, None) for copy in gather_side(p, shard(j), order[j], wsems))
 
     def far(j):
-        going.extend((copy, None) for copy in gather_far(p, buf, order[j], wsems))
+        going.extend((copy, None) for copy in gather_far(p, shard(j), order[j], wsems))
 
     loads[0].wait()
-    k.slots[pl.ds(slot_dev * p.z, slot_dev), p.n] = k.weight_v[...].astype(bf16)
+    k.slots[pl.ds(slot_dev * p.z, slot_dev), p.n // 2, p.c] = k.weight_v[...].astype(bf16)
     greet_end(depth, peers)
 
     def rounds(*names):
         for name in names:
-            {"a": arrive, "s": side, "f": far}[name[0]](int(name[1:]))
-
+            i = int(name[1:])
+            if name[0] == "b":
+                rest_pass(i // slot_dev, i % slot_dev)
+            else:
+                {"a": arrive, "s": side, "f": far}[name[0]](i)
+
+    rest_start(slot_dev - 1)
     rounds("a0", "a1")
     loads[1].wait()
     node_ids = lax.broadcasted_iota(jnp.int32, (nodes, halo), 0)
@@ -492,39 +546,38 @@
     k.hput[...] = k.spread[...].reshape(peers, roll * per_peer, width).astype(bf16)
     k.halo[p.n] = k.hput[p.n]
     rounds("a2", "a3", "s0", "s1")
-    hsent = []
-    for i in range(1, peers):
-        to = lax.rem(p.n + i, peers)
-        hsent.append(remote(k.hput.at[to], k.halo.at[p.n], k.h_send.at[0, i], k.h_recv.at[0, i], p.z, to))
-        hsent[-1].start()
     loads[2].wait()
     for s in range(slot_dev):
         k.pre[2 * slot_dev + s, p.n] = k.grad[2, s].astype(bf16)
         for m in range(peers):
             k.lput[s, m] = k.grad[2, s, :, m * rows : (m + 1) * rows].astype(bf16)
     k.lgot[:, p.n] = k.lput[:, p.n]
-    rounds("a4", "a5", "s2", "s3", "f0", "f1")
+    rounds("a4", "a5", "s2", "s3", "b1", "f0", "f1")
     ids = lax.broadcasted_iota(jnp.int32, (padded, edges), 0)
     onehot = (ids == k.sender_ref[...].reshape(1, edges)) | (
         ids == k.receiver_ref[...].reshape(1, edges) + known
     )
     onehot = jnp.where(onehot, 1.0, 0.0).astype(f32)
     k.gather_t[...] = onehot.astype(bf16)
-    rounds("a6", "a7", "s4", "s5", "f2", "f3")
+    rounds("a6", "a7", "s4", "s5", "b3", "f2", "f3")
     k.gather[...] = onehot.T.astype(bf16)
     k.table[:, known + nodes :] = jnp.zeros((roll, padded - known - nodes, width), bf16)
     k.acc[...] = jnp.zeros_like(k.acc)
-    rounds("s6", "s7", "f4", "f5")
+    rounds("s6", "s7")
+    hsent = []
+    for i in range(1, peers):
+        to = lax.rem(p.n + i, peers)
+        hsent.append(remote(k.hput.at[to], k.halo.at[p.n], k.h_send.at[0, i], k.h_recv.at[0, i], p.z, to))
+        hsent[-1].start()
+    rounds("b5", "f4", "f5", "b7")
     loads[3].wait()
     for s in range(slot_dev):
         k.right_b[s] = k.grad[s].reshape(width, width).astype(bf16)
     rounds("f6", "f7")
-    for copy in hsent:
-        copy.wait_send()
-    for i in range(1, peers):
-        landed(k.halo.at[0], k.h_recv.at[0, i])
-    for slot in order:
-        gather_end(p, buf, slot, wsems)
+    for j, slot in enumerate(order):
+        gather_end(p, shard(j), slot, wsems)
+        if j % slot_dev == slot_dev - 1:
+            rest_end(slot)
 
     slot_of = []
     for b in range(NBLOCK):
@@ -547,6 +600,10 @@
 
     own_sent = dot(flat_nodes(), weight(1))
     own_recv = dot(flat_nodes(), weight(2))
+    for copy in hsent:
+        copy.wait_send()
+    for i in range(1, peers):
+        landed(k.halo.at[0], k.h_recv.at[0, i])
     halo_flat = k.halo[...].reshape(roll * halo, width)
     halo_sent = dot(halo_flat, weight(1)).reshape(peers, roll, per_peer, width)
     for t in range(roll):
@@ -702,12 +759,18 @@
 
     lax.fori_loop(0, roll, backward, 0)
 
+    def kept(i):
+        return k.table[:, i * nodes : (i + 1) * nodes].reshape(roll * nodes, width)
+
+    def edge_gradient(t):
+        for c in range(pieces):
+            at = pl.ds(c * chunk, chunk)
+            grown = k.egrad_v[0, t, at].astype(f32) + dot_tb(k.slope_v[t, at], weight(0))
+            k.egrad_v[0, t, at] = grown.astype(bf16)
+
     to_core(3)
     to_core(0)
     k.hput[...] = k.spread[...].reshape(peers, roll * per_peer, width).astype(bf16)
-    def kept(i):
-        return k.table[:, i * nodes : (i + 1) * nodes].reshape(roll * nodes, width)
-
     put_grad(1, dot_ta(flat_nodes(), kept(0)) + dot_ta(halo_flat, k.hput[...].reshape(roll * halo, width)))
     to_core(1)
     to_first(3)
@@ -725,13 +788,6 @@
     to_second(0)
     for i in early:
         going.extend((copy, None) for copy in gather_far(p, pbuf, i, psems))
-
-    def edge_gradient(t):
-        for c in range(pieces):
-            at = pl.ds(c * chunk, chunk)
-            grown = k.egrad_v[0, t, at].astype(f32) + dot_tb(k.slope_v[t, at], weight(0))
-            k.egrad_v[0, t, at] = grown.astype(bf16)
-
     to_second(1)
     settle(3)
     to_second(2)
@@ -751,13 +807,29 @@
         held = k.grad[jnp.minimum(b, NBLOCK - 1), p.n]
         return jnp.where(b < NBLOCK, held, 0.0)
 
+    last = depth - 1
+
+    def z_hop(way, target, s, to):
+        put, got = (k.put_up, k.got_up) if way == 0 else (k.put_down, k.got_down)
+        return remote(
+            put.at[target, s], got.at[target, s], k.z_send.at[way, target, s], k.z_recv.at[way, target, s], to, p.n
+        )
+
+    def far_hop(s):
+        return remote(k.put_far.at[s], k.got_far.at[s], k.f_send.at[s], k.f_recv.at[s], last - p.z, p.n)
+
     def pass_on(way):
         put, got = (k.put_up, k.got_up) if way == 0 else (k.put_down, k.got_down)
-        source = p.z > 0 if way == 0 else p.z < depth - 1
-        for i in range(depth - 1):
-            target = depth - 1 - i if way == 0 else i
+        to = p.z + 1 if way == 0 else p.z - 1
+        for step in (last, last - 1, 1):
+            target = step if way == 0 else last - step
             test = p.z < target if way == 0 else p.z > target
-            at = p.z + 1 if way == 0 else p.z - 1
+            if step == last:
+                end = last if way == 0 else 0
+                test = test & (p.z != last - end)
+                source = (p.z != last - end) & (p.z != (1 if way == 0 else last - 1))
+            else:
+                source = p.z > 0 if way == 0 else p.z < last
 
             @pl.when(test)
             def _():
@@ -765,7 +837,7 @@
 
                     @pl.when(source)
                     def _():
-                        landed(got.at[target, s], k.z_recv.at[way, target, s])
+                        z_hop(way, target, s, to).wait_recv()
                         total = part(target, s) + got[target, s].astype(f32)
                         put[target, s] = total.astype(bf16)
 
@@ -773,14 +845,15 @@
                     def _():
                         put[target, s] = part(target, s).astype(bf16)
 
-                    remote(
-                        put.at[target, s],
-                        got.at[target, s],
-                        k.z_send.at[way, target, s],
-                        k.z_recv.at[way, target, s],
-                        at,
-                        p.n,
-                    ).start()
+                    z_hop(way, target, s, to).start()
+
+            if step == last - 1:
+
+                @pl.when(p.z == (0 if way == 0 else last))
+                def _():
+                    for s in range(slot_dev):
+                        k.put_far[s] = part(last - p.z, s).astype(bf16)
+                        far_hop(s).start()
 
     @pl.when(p.z == 0)
     def _():
@@ -832,6 +905,12 @@
 
         mine = part(p.z, s) + jnp.where(p.z > 0, k.got_up[p.z, s].astype(f32), 0.0)
         mine = mine + jnp.where(p.z < depth - 1, k.got_down[p.z, s].astype(f32), 0.0)
+
+        @pl.when((p.z == 0) | (p.z == last))
+        def _():
+            far_hop(s).wait_recv()
+
+        mine = mine + jnp.where((p.z == 0) | (p.z == last), k.got_far[s].astype(f32), 0.0)
         k.full[s, p.n] = mine.astype(bf16)
         for copy in gather_start(p, gbuf, s, gsems):
             going.append((copy, None))
@@ -844,9 +923,10 @@
         launch(k.sput, k.sgot.at[p.n], k.n_send.at[i], k.n_recv.at[i], p.z, to)
     edge_gradient(3)
 
-    def collect(buffer, sems, finish):
+    def collect(buffer, sems, between, finish):
         for s in range(slot_dev):
             going.extend((copy, None) for copy in gather_side(p, buffer, s, sems))
+        between()
         for s in range(slot_dev):
             going.extend((copy, None) for copy in gather_far(p, buffer, s, sems))
         for s in range(slot_dev):
@@ -863,16 +943,6 @@
 
     limit = math.sqrt(NBLOCK * width * width + 8 * width)
     found = []
-
-    for i in range(1, peers):
-        landed(k.hret.at[0], k.h_recv.at[1, i])
-    back = k.hret[...].astype(f32).reshape(peers, roll, per_peer, width)
-    for t in range(roll):
-        rows_t = back[:, t].reshape(halo, width).astype(bf16)
-        k.table[t, :nodes] = (k.table[t, :nodes].astype(f32) + dot(pick_t, rows_t)).astype(bf16)
-    grown = k.ncot_v[...].reshape(roll * nodes, width).astype(f32) * row_live
-    grown = grown + dot_tb(kept(0), weight(1)) + dot_tb(kept(1), weight(2)) + dot_tb(kept(2), weight(4))
-    k.ngrad_v[0] = grown.astype(bf16).reshape(roll, nodes, width)
 
     def fix(beta, step):
         return 1.0 - jnp.exp2(math.log2(beta) * jnp.full((1, 1), step, jnp.int32).astype(f32))
@@ -924,7 +994,18 @@
         landed(k.lgot.at[:, 0], k.l_recv.at[i])
     for i in early:
         gather_end(p, pbuf, i, psems)
-    collect(gbuf, gsems, advance)
+    def node_gradient():
+        for i in range(1, peers):
+            landed(k.hret.at[0], k.h_recv.at[1, i])
+        back = k.hret[...].astype(f32).reshape(peers, roll, per_peer, width)
+        for t in range(roll):
+            rows_t = back[:, t].reshape(halo, width).astype(bf16)
+            k.table[t, :nodes] = (k.table[t, :nodes].astype(f32) + dot(pick_t, rows_t)).astype(bf16)
+        grown = k.ncot_v[...].reshape(roll * nodes, width).astype(f32) * row_live
+        grown = grown + dot_tb(kept(0), weight(1)) + dot_tb(kept(1), weight(2)) + dot_tb(kept(2), weight(4))
+        k.ngrad_v[0] = grown.astype(bf16).reshape(roll, nodes, width)
+
+    collect(gbuf, gsems, node_gradient, advance)
     grad_vectors, clip = found
     step = k.step_ref[depth * slot_dev]
     spun = grad_vectors * clip
@@ -944,21 +1025,16 @@
     for b in range(NBLOCK):
         for stage in range(3):
             hop(stage, b).wait_send()
-    for i in range(depth - 1):
-        for s in range(slot_dev):
-            for test, target, way, put in (
-                (p.z < depth - 1 - i, depth - 1 - i, 0, k.put_up),
-                (p.z > i, i, 1, k.put_down),
-            ):
-                sent = remote(
-                    put.at[target, s],
-                    put.at[target, s],
-                    k.z_send.at[way, target, s],
-                    k.z_recv.at[way, target, s],
-                    p.z,
-                    p.sib,
-                )
-                pl.when(test)(sent.wait_send)
+    for way in range(2):
+        for step in (last, last - 1, 1):
+            target = step if way == 0 else last - step
+            test = p.z < target if way == 0 else p.z > target
+            if step == last:
+                test = test & (p.z != last - target)
+            for s in range(slot_dev):
+                pl.when(test)(z_hop(way, target, s, lax.rem(p.z + 1, depth)).wait_send)
+    for s in range(slot_dev):
+        pl.when((p.z == 0) | (p.z == last))(far_hop(s).wait_send)
 
 
 def store_kernel(*refs):
@@ -1045,7 +1121,7 @@
         node_v=v((roll, nodes, width), bf16),
         edge_v=v((roll, edges, width), bf16),
         ncot_v=v((roll, nodes, width), bf16),
-        slots=v((slot_dev * depth, peers, rows, width), bf16),
+        slots=v((slot_dev * depth, peers // 2, 2, rows, width), bf16),
         halo=v((peers, roll * per_peer, width), bf16),
         spread=v((peers, roll, per_peer, width), f32),
         hput=v((peers, roll * per_peer, width), bf16),
@@ -1074,6 +1150,8 @@
         put_down=v((depth, *own), bf16),
         got_up=v((depth, *own), bf16),
         got_down=v((depth, *own), bf16),
+        put_far=v(own, bf16),
+        got_far=v(own, bf16),
         full=v((slot_dev, peers, rows, width), bf16),
         vput=v((4, 8, width), f32),
         vgot=v((3, 8, width), f32),
@@ -1085,8 +1163,14 @@
         in_sem=dma((9,)),
         w_send=dma((7, depth * slot_dev)),
         w_recv=dma((7, depth * slot_dev)),
-        wz_send=dma((2, depth * slot_dev)),
+        wz_send=dma((3, depth * slot_dev)),
         wz_recv=dma((depth * slot_dev,)),
+        b_send=dma((3, slot_dev)),
+        b_recv=dma((3, slot_dev)),
+        bz_send=dma((3, depth * slot_dev)),
+        bz_recv=dma((depth * slot_dev,)),
+        bs_send=dma((depth * slot_dev,)),
+        bs_recv=dma((depth * slot_dev,)),
         h_send=dma((2, peers)),
         h_recv=dma((2, peers)),
         l_send=dma((peers,)),
@@ -1095,6 +1179,8 @@
         r_recv=dma((3 * NBLOCK,)),
         z_send=dma((2, depth, slot_dev)),
         z_recv=dma((2, depth, slot_dev)),
+        f_send=dma((slot_dev,)),
+        f_recv=dma((slot_dev,)),
         g_send=dma((7, slot_dev)),
         g_recv=dma((7, slot_dev)),
         p_send=dma((7, 3 * slot_dev)),

time: 116 us -> 109 us (0.940)
  Pallas kernels: 114 us -> 108 us
    pallas_call x1, Pallas kernels: 110 us -> 104 us  [whole_step(): pl.pallas_call(functools.partial(step_kernel, names), out_shape=tuple((pl...]
where the time goes in v4:
time: 109 us
  Pallas kernels  108 us (99%)
  between operations  1.46 us (1%)
    pallas_call x1, Pallas kernels, whole_step(): pl.pallas_call(functools.partial(step_kernel, names), out_shape=tuple((pl...  104 us
    pallas_call x1, Pallas kernels, whole_step(): pl.pallas_call(store_kernel, out_shape=(*final, shape((1,), f32)), in_spe...  3.83 us

profile of v4, /device:TPU:1, one launch (start us, length us, event | category | flops | bytes accessed | tf_op | source)
XLA Modules:
  0.0 109.0 jit_solution(7204981174198233986)
XLA Ops:
  1.3 103.7 %step.1 = (bf16[1,4,128,512]{3,2,1,0:T(8,128)(2,1)S(1)}, bf16[1,4,768,512]{3,2,1,0:T(8,128)(2,1)S(1)}, bf16[1,4,128,512]{3,2,1,0:T(8,128)(2,1)S(1)}, bf16[1,4,76...) custom-call(s32[1]{0:T(128)S(6)} %copy.28.refs_0_, ...), custom_call_target="tpu_custom_call" | custom-call | tf_op jit(solution)/shard_map/step/pallas_call | solution.py:1194
  105.0 3.8 %results.1 = (bf16[1,4,128,512]{3,2,1,0:T(8,128)(2,1)}, bf16[1,4,768,512]{3,2,1,0:T(8,128)(2,1)}, bf16[1,4,128,512]{3,2,1,0:T(8,128)(2,1)}, bf16[1,4,768,512]{3,...) custom-call(bf16[1,4,128,512]{3,2,1,0:T(8,128)(2,1)S(1)} %get-tuple-, ...), custom_call_target="tpu_custom_call" | custom-call | tf_op jit(solution)/shard_map/results/pallas_call | solution.py:1211

commit v5 on v4

--- a/solution.py
+++ b/solution.py
@@ -368,7 +368,7 @@
     return copies
 
 
-def gather_side(p, buf, k, sems):
+def gather_side(p, buf, k, sems, over_far=True):
     send, recv = sems
     copies = []
     for i, owner in ((0, p.xn), (1, p.yn)):
@@ -377,9 +377,11 @@
         on = remote(got, got, send.at[4 + i, k], recv.at[4 + i, k], p.z, p.sib)
         on.start()
         copies.append(on)
-        over = remote(got, got, send.at[2, k], recv.at[2, k], p.z, p.yn if i == 0 else p.xn)
-        pl.when(p.c == i)(over.start)
-    copies.append(over)
+        if over_far:
+            over = remote(got, got, send.at[2, k], recv.at[2, k], p.z, p.yn if i == 0 else p.xn)
+            pl.when(p.c == i)(over.start)
+    if over_far:
+        copies.append(over)
     return copies
 
 
@@ -644,7 +646,8 @@
         k.summed_v[pl.ds(t * nodes, nodes)] = total.astype(bf16)
         return carry
 
-    lax.fori_loop(0, roll, forward, 0)
+    for t in range(roll):
+        forward(t, 0)
 
     on_f = jnp.where(p.c == 0, p.x, p.y)
     on_g = jnp.where(p.c == 0, p.y, p.x)
@@ -914,6 +917,7 @@
         k.full[s, p.n] = mine.astype(bf16)
         for copy in gather_start(p, gbuf, s, gsems):
             going.append((copy, None))
+        launch(gbuf(s, p.n), gbuf(s, p.n), k.g_send.at[2, s], k.g_recv.at[2, s], p.z, p.diag)
         square = square + eights(mine * mine)
     square = square[:, :128] + square[:, 128:256] + square[:, 256:384] + square[:, 384:]
     k.sput[...] = square
@@ -925,10 +929,10 @@
 
     def collect(buffer, sems, between, finish):
         for s in range(slot_dev):
-            going.extend((copy, None) for copy in gather_side(p, buffer, s, sems))
-        between()
+            going.extend((copy, None) for copy in gather_side(p, buffer, s, sems, False))
         for s in range(slot_dev):
             going.extend((copy, None) for copy in gather_far(p, buffer, s, sems))
+        between()
         for s in range(slot_dev):
             gather_end(p, buffer, s, sems)
             finish(s)

time: 109 us -> 109 us (level); the launches traced: 109 us -> 107 us
  Pallas kernels: 108 us -> 106 us
    pallas_call x1, Pallas kernels: 104 us -> 102 us  [whole_step(): pl.pallas_call(functools.partial(step_kernel, names), out_shape=tuple((pl...]
where the time goes in v5:
time: 109 us; the launch traced here: 107 us
  Pallas kernels  106 us (97%)
  between operations  1.48 us (1%)
    pallas_call x1, Pallas kernels, whole_step(): pl.pallas_call(functools.partial(step_kernel, names), out_shape=tuple((pl...  102 us
    pallas_call x1, Pallas kernels, whole_step(): pl.pallas_call(store_kernel, out_shape=(*final, shape((1,), f32)), in_spe...  3.83 us

profile of v5, /device:TPU:1, one launch (start us, length us, event | category | flops | bytes accessed | tf_op | source)
XLA Modules:
  0.0 107.1 jit_solution(12437321989975040541)
XLA Ops:
  1.3 101.8 %step.1 = (bf16[1,4,128,512]{3,2,1,0:T(8,128)(2,1)S(1)}, bf16[1,4,768,512]{3,2,1,0:T(8,128)(2,1)S(1)}, bf16[1,4,128,512]{3,2,1,0:T(8,128)(2,1)S(1)}, bf16[1,4,76...) custom-call(s32[1]{0:T(128)S(6)} %copy.28.refs_0_, ...), custom_call_target="tpu_custom_call" | custom-call | tf_op jit(solution)/shard_map/step/pallas_call | solution.py:1198
  103.1 3.8 %results.1 = (bf16[1,4,128,512]{3,2,1,0:T(8,128)(2,1)}, bf16[1,4,768,512]{3,2,1,0:T(8,128)(2,1)}, bf16[1,4,128,512]{3,2,1,0:T(8,128)(2,1)}, bf16[1,4,768,512]{3,...) custom-call(bf16[1,4,128,512]{3,2,1,0:T(8,128)(2,1)S(1)} %get-tuple-, ...), custom_call_target="tpu_custom_call" | custom-call | tf_op jit(solution)/shard_map/results/pallas_call | solution.py:1215

commit v6 on v5

--- a/solution.py
+++ b/solution.py
@@ -505,6 +505,8 @@
     wsems = (k.w_send, k.w_recv)
     order = []
 
+    straight = depth * slot_dev - 1
+
     def arrive(j):
         z_of = planes[j // slot_dev]
         slot = z_of * slot_dev + j % slot_dev
@@ -519,9 +521,11 @@
             pl.when(test)(copy.start)
             going.append((copy, test))
         going.extend((copy, None) for copy in gather_start(p, shard(j), slot, wsems))
+        if j >= straight:
+            launch(piece, piece, k.w_send.at[2, slot], k.w_recv.at[2, slot], p.z, p.diag)
 
     def side(j):
-        going.extend((copy, None) for copy in gather_side(p, shard(j), order[j], wsems))
+        going.extend((copy, None) for copy in gather_side(p, shard(j), order[j], wsems, j < straight))
 
     def far(j):
         going.extend((copy, None) for copy in gather_far(p, shard(j), order[j], wsems))

time: 109 us -> 108 us (level)
  no operation moved by 1% of the time
where the time goes in v6:
time: 108 us; the launch traced here: 106 us
  Pallas kernels  105 us (97%)
  between operations  1.48 us (1%)
    pallas_call x1, Pallas kernels, whole_step(): pl.pallas_call(functools.partial(step_kernel, names), out_shape=tuple((pl...  101 us
    pallas_call x1, Pallas kernels, whole_step(): pl.pallas_call(store_kernel, out_shape=(*final, shape((1,), f32)), in_spe...  3.83 us

profile of v6, /device:TPU:1, one launch (start us, length us, event | category | flops | bytes accessed | tf_op | source)
XLA Modules:
  0.0 106.4 jit_solution(15525059605836169427)
XLA Ops:
  1.3 101.1 %step.1 = (bf16[1,4,128,512]{3,2,1,0:T(8,128)(2,1)S(1)}, bf16[1,4,768,512]{3,2,1,0:T(8,128)(2,1)S(1)}, bf16[1,4,128,512]{3,2,1,0:T(8,128)(2,1)S(1)}, bf16[1,4,76...) custom-call(s32[1]{0:T(128)S(6)} %copy.28.refs_0_, ...), custom_call_target="tpu_custom_call" | custom-call | tf_op jit(solution)/shard_map/step/pallas_call | solution.py:1202
  102.4 3.8 %results.1 = (bf16[1,4,128,512]{3,2,1,0:T(8,128)(2,1)}, bf16[1,4,768,512]{3,2,1,0:T(8,128)(2,1)}, bf16[1,4,128,512]{3,2,1,0:T(8,128)(2,1)}, bf16[1,4,768,512]{3,...) custom-call(bf16[1,4,128,512]{3,2,1,0:T(8,128)(2,1)S(1)} %get-tuple-, ...), custom_call_target="tpu_custom_call" | custom-call | tf_op jit(solution)/shard_map/results/pallas_call | solution.py:1219
